TPU v7x, 32 devices: a whole 2x2x4 slice. The times are simulated.
32 devices in a mesh: dp: 8 (over z, y), mp: 4 (over x, core).
Axes of the slice: x: 2, y: 2, z: 4, core: 2. Of those that a mesh axis runs over, the one named last changes fastest.
Arguments:
- tokens: bfloat16 [32768, 768], P('dp'), may hold values from -6 to 6
- cotangent: bfloat16 [32768, 768], P('dp'), may hold values from -6 to 6
- attention_norm_gain: bfloat16 [768], replicated, may hold values from 0.099609375 to 1.8984375
- feedforward_norm_gain: bfloat16 [768], replicated, may hold values from 0.099609375 to 1.8984375
- query_projection_weight: bfloat16 [768, 768], P(None, 'mp'), may hold values from -0.03125 to 0.03125
- key_value_weight: bfloat16 [2, 768, 768], P(None, None, 'mp'), may hold values from -0.21875 to 0.21875
- attention_output_weight: bfloat16 [768, 768], P('mp'), may hold values from -0.625 to 0.625
- ffn_input_weight: bfloat16 [768, 3072], P(None, 'mp'), may hold values from -0.21875 to 0.21875
- ffn_output_weight: bfloat16 [3072, 768], P('mp'), may hold values from -0.109375 to 0.109375
- projection_down_weight: bfloat16 [3, 768, 40], replicated, may hold values from -0.21875 to 0.21875
- query_up_weight: bfloat16 [40, 768], P(None, 'mp'), may hold values from -1.5 to 1.5
- key_value_up_weight: bfloat16 [2, 40, 768], P(None, None, 'mp'), may hold values from -9 to 9
- attention_output_down_weight: bfloat16 [768, 40], replicated, may hold values from -0.625 to 0.625
- attention_output_up_weight: bfloat16 [40, 768], replicated, may hold values from -9 to 9
- ffn_input_down_weight: bfloat16 [768, 40], replicated, may hold values from -0.21875 to 0.21875
- ffn_input_up_weight: bfloat16 [40, 3072], P(None, 'mp'), may hold values from -9 to 9
- ffn_output_down_weight: bfloat16 [3072, 40], replicated, may hold values from -0.109375 to 0.109375
- ffn_output_up_weight: bfloat16 [40, 768], replicated, may hold values from -12 to 12
- attention_router_weight: bfloat16 [768, 10], replicated, may hold values from -0.109375 to 0.109375
- feedforward_router_weight: bfloat16 [768, 10], replicated, may hold values from -0.109375 to 0.109375
- bucket_bias_table: bfloat16 [32, 12], P(None, 'mp'), may hold values from -3 to 3
- offset_bucket_map: int32 [1023], replicated, may hold values from 0 to 31
- sequence_length_list: int32 [160], P('dp'), may hold values from 32 to 512, as said below
Outputs:
- output: bfloat16 [32768, 768], P('dp')
- grad_tokens: bfloat16 [32768, 768], P('dp')
- grad_attn_gain: float32 [768], replicated
- grad_ffn_gain: float32 [768], replicated
- grad_lora_a_qkv: float32 [3, 768, 40], replicated
- grad_lora_b_query: float32 [40, 768], P(None, 'mp')
- grad_lora_b_keyval: float32 [2, 40, 768], P(None, None, 'mp')
- grad_lora_a_out: float32 [768, 40], replicated
- grad_lora_b_out: float32 [40, 768], replicated
- grad_lora_a_in: float32 [768, 40], replicated
- grad_lora_b_in: float32 [40, 3072], P(None, 'mp')
- grad_lora_a_ffout: float32 [3072, 40], replicated
- grad_lora_b_ffout: float32 [40, 768], replicated
- grad_router_attn: float32 [768, 10], replicated
- grad_router_ffn: float32 [768, 10], replicated
- grad_bias_table: float32 [32, 12], P(None, 'mp')
Inputs may be any that keep to these rules, and one draw needn't show every extreme that they name: `sequence_length_list`: block by block of 20: 16 lengths of short sequences, the first equal to 128 and the others from 32 to 128, then 4 lengths of long sequences from 128 to 512; the first long sequence of every fourth block has length 512.
All inputs are finite; a program needn't handle non-finite values.
Results may differ from a plain program's by a relative error of at most 0.022.
The roundings to bfloat16 on the way count: a program that leaves them out, or rounds other values in their place, can miss the bound.
Values may be sent and summed in bfloat16 or wider, within the bound.
No kernel may reach another device: no remote copies, remote signals or barrier semaphores. Data moves between devices by JAX's collectives and lax.ppermute only.
A program may use at most 320 MiB of HBM per device.

v0:
```python
import jax
import jax.numpy as jnp
from jax import lax
from jax.sharding import PartitionSpec as P

HEAD_WIDTH = 64
BUCKETS = 32
ADAPTER_RANK = 4
SHORT_LEN = 128
LONG_LEN = 512
LONG_SEQS = 4
SHORT_SEQS = 16


eps_norm = 1e-06
brain_float = jnp.bfloat16
single_precision = jnp.float32
highest = lax.Precision.HIGHEST


def matrix_product(left_op, right_op):
    return jnp.dot(left_op, right_op, preferred_element_type=single_precision)


def contract_rows(left_op, right_op):
    return lax.dot_general(
        left_op, right_op, (((0,), (0,)), ((), ())), preferred_element_type=single_precision
    )


def product_with_transpose(left_op, right_op):
    return lax.dot_general(
        left_op, right_op, (((1,), (1,)), ((), ())), preferred_element_type=single_precision
    )


def per_expert(values):
    return values.reshape(values.shape[0], -1, ADAPTER_RANK).sum(-1)


def spread_gates(gate_probs):
    return jnp.repeat(gate_probs, ADAPTER_RANK, axis=1)


def norm_forward(values, gain_vec):
    inv_rms = lax.rsqrt(jnp.mean(values * values, -1, keepdims=True) + eps_norm)
    return (values * inv_rms * gain_vec, inv_rms)


def norm_backward(values, inv_rms, gain_vec, grad_normed):
    weighted = grad_normed * gain_vec
    inner_term = jnp.mean(weighted * values, -1, keepdims=True)
    return inv_rms * weighted - values * inv_rms * inv_rms * inv_rms * inner_term


def softmax_backward(gate_probs, grad_gates):
    return gate_probs * (grad_gates - jnp.sum(gate_probs * grad_gates, -1, keepdims=True))


def silu_slope(values):
    sigmoid_part = jax.nn.sigmoid(values)
    return sigmoid_part * (1.0 + values * (1.0 - sigmoid_part))


def score_block(query_matrix_rows, key_matrix_rows, pos_bias, lengths, seq_span):
    scores = jnp.einsum(
        "sqhd,skhd->shqk",
        query_matrix_rows,
        key_matrix_rows,
        preferred_element_type=single_precision,
    )
    scores = scores + pos_bias[None, :, :seq_span, :seq_span]
    positions = jnp.arange(seq_span, dtype=jnp.int32)
    key_valid = positions[None, :] < lengths[:, None]
    return jnp.where(key_valid[:, None, None, :], scores, -1000000000.0)


def attend_forward(
    query_matrix_rows, key_matrix_rows, value_matrix_rows, pos_bias, lengths, seq_span
):
    scores = score_block(query_matrix_rows, key_matrix_rows, pos_bias, lengths, seq_span)
    row_peak = jnp.max(scores, -1, keepdims=True)
    row_total = jnp.sum(jnp.exp(scores - row_peak), -1, keepdims=True)
    log_total = row_peak + jnp.log(row_total)
    weight_collection = jnp.exp(scores - log_total).astype(brain_float)
    attended_rows = jnp.einsum(
        "shqk,skhd->sqhd",
        weight_collection,
        value_matrix_rows,
        preferred_element_type=single_precision,
    )
    return (attended_rows, log_total)


def attend_backward(
    query_matrix_rows,
    key_matrix_rows,
    value_matrix_rows,
    pos_bias,
    lengths,
    seq_span,
    log_total,
    grad_attended,
):
    scores = score_block(query_matrix_rows, key_matrix_rows, pos_bias, lengths, seq_span)
    attn_probs = jnp.exp(scores - log_total)
    grad_probs = jnp.einsum(
        "sqhd,skhd->shqk", grad_attended, value_matrix_rows, preferred_element_type=single_precision
    )
    grad_values = jnp.einsum(
        "shqk,sqhd->skhd",
        attn_probs.astype(brain_float),
        grad_attended,
        preferred_element_type=single_precision,
    )
    grad_scores = attn_probs * (grad_probs - jnp.sum(attn_probs * grad_probs, -1, keepdims=True))
    grad_scores = grad_scores.astype(brain_float)
    grad_queries = jnp.einsum(
        "shqk,skhd->sqhd", grad_scores, key_matrix_rows, preferred_element_type=single_precision
    )
    grad_keys = jnp.einsum(
        "shqk,sqhd->skhd", grad_scores, query_matrix_rows, preferred_element_type=single_precision
    )
    bias_part = jnp.sum(grad_scores.astype(single_precision), 0)
    return (grad_queries, grad_keys, grad_values, bias_part)


def table_grad(bias_part, seq_span, onehot):
    head_count = bias_part.shape[0]
    flipped = bias_part[:, ::-1, :]
    padded = jnp.concatenate([flipped, jnp.zeros_like(flipped)], 2)
    skewed = padded.reshape(head_count, -1)[:, : seq_span * (2 * seq_span - 1)]
    skewed = skewed.reshape(head_count, seq_span, 2 * seq_span - 1)
    by_offset = jnp.sum(skewed, 1)
    chosen = onehot[LONG_LEN - seq_span : LONG_LEN + seq_span - 1]
    return lax.dot_general(
        chosen,
        by_offset,
        (((0,), (1,)), ((), ())),
        precision=highest,
        preferred_element_type=single_precision,
    )


def attention_half(block_of_rows, lengths, seq_count, seq_span, weight_collection, pos_bias):
    (
        attention_norm_gain,
        query_projection_weight,
        key_value_weight,
        attention_output_weight,
        down_joined,
        query_up_weight,
        key_value_up_weight,
        attention_output_down_rows,
        attention_output_up_weight,
        attention_router_weight,
    ) = weight_collection
    normed_full, inv_rms = norm_forward(block_of_rows, attention_norm_gain.astype(single_precision))
    first_normalized = normed_full.astype(brain_float)
    gate_probs = jax.nn.softmax(matrix_product(first_normalized, attention_router_weight), axis=-1)
    spread_one = spread_gates(gate_probs)
    rank_columns = spread_one.shape[1]
    down_qkv = matrix_product(first_normalized, down_joined)
    blended_projection = (jnp.tile(spread_one, (1, 3)) * down_qkv).astype(brain_float)
    query_matrix_rows = (
        matrix_product(first_normalized, query_projection_weight)
        + matrix_product(blended_projection[:, :rank_columns], query_up_weight)
    ).astype(brain_float)
    key_matrix_rows = (
        matrix_product(first_normalized, key_value_weight[0])
        + matrix_product(
            blended_projection[:, rank_columns : 2 * rank_columns], key_value_up_weight[0]
        )
    ).astype(brain_float)
    value_matrix_rows = (
        matrix_product(first_normalized, key_value_weight[1])
        + matrix_product(blended_projection[:, 2 * rank_columns :], key_value_up_weight[1])
    ).astype(brain_float)
    blocked = (seq_count, seq_span, query_matrix_rows.shape[1] // HEAD_WIDTH, HEAD_WIDTH)
    attended_rows, log_total = attend_forward(
        query_matrix_rows.reshape(blocked),
        key_matrix_rows.reshape(blocked),
        value_matrix_rows.reshape(blocked),
        pos_bias,
        lengths,
        seq_span,
    )
    attended_rows = attended_rows.reshape(block_of_rows.shape[0], -1).astype(brain_float)
    output_total, down_out = lax.psum(
        (
            matrix_product(attended_rows, attention_output_weight),
            matrix_product(attended_rows, attention_output_down_rows),
        ),
        "mp",
    )
    blended_output = (spread_one * down_out).astype(brain_float)
    hidden_units_rows = block_of_rows + (
        output_total + matrix_product(blended_output, attention_output_up_weight)
    )
    return {
        "normed": first_normalized,
        "scale": inv_rms,
        "gates": gate_probs,
        "spread": spread_one,
        "down_qkv": down_qkv,
        "mixed_qkv": blended_projection,
        "queries": query_matrix_rows,
        "keys": key_matrix_rows,
        "values": value_matrix_rows,
        "log_total": log_total,
        "attended": attended_rows,
        "down_out": down_out,
        "mixed_out": blended_output,
        "hidden": hidden_units_rows,
    }


def ffn_local(hidden_units_rows, weight_collection):
    (
        feedforward_norm_gain,
        ffn_input_weight,
        ffn_input_down_weight,
        ffn_input_up_weight,
        feedforward_router_weight,
        ffn_output_weight,
        ffn_output_down_rows,
        ffn_output_up_weight,
    ) = weight_collection
    normed_full, inv_rms = norm_forward(
        hidden_units_rows, feedforward_norm_gain.astype(single_precision)
    )
    second_normalized = normed_full.astype(brain_float)
    gate_probs = jax.nn.softmax(
        matrix_product(second_normalized, feedforward_router_weight), axis=-1
    )
    spread_two = spread_gates(gate_probs)
    input_down_rows = matrix_product(second_normalized, ffn_input_down_weight)
    blended_input = (spread_two * input_down_rows).astype(brain_float)
    before_residual = matrix_product(second_normalized, ffn_input_weight) + matrix_product(
        blended_input, ffn_input_up_weight
    )
    active_values = jax.nn.silu(before_residual).astype(brain_float)
    return {
        "normed": second_normalized,
        "scale": inv_rms,
        "gates": gate_probs,
        "spread": spread_two,
        "down": input_down_rows,
        "mixed": blended_input,
        "before": before_residual,
        "active": active_values,
    }


def ffn_back(ffn_state, down_ff, hidden_units_rows, gradient_output_rows, weight_collection):
    (
        feedforward_norm_gain,
        ffn_input_weight,
        ffn_input_down_weight,
        ffn_input_up_weight,
        feedforward_router_weight,
        ffn_output_weight,
        ffn_output_down_rows,
        ffn_output_up_weight,
    ) = weight_collection
    spread_two = ffn_state["spread"]
    blended_feedforward = (spread_two * down_ff).astype(brain_float)
    adapter_feedforward_delta = product_with_transpose(gradient_output_rows, ffn_output_up_weight)
    grad_ffout_up = contract_rows(blended_feedforward, gradient_output_rows)
    gate_grad = per_expert(down_ff * adapter_feedforward_delta)
    grad_down_ff = (spread_two * adapter_feedforward_delta).astype(brain_float)
    gradient_ffn_output_down = contract_rows(ffn_state["active"], grad_down_ff)
    grad_active = (
        product_with_transpose(gradient_output_rows, ffn_output_weight)
        + product_with_transpose(grad_down_ff, ffn_output_down_rows)
    ).astype(brain_float)
    gradient_before_residual = (
        silu_slope(ffn_state["before"]) * grad_active.astype(single_precision)
    ).astype(brain_float)
    grad_in_up = contract_rows(ffn_state["mixed"], gradient_before_residual)
    normed_sum, side_in = lax.psum(
        (
            product_with_transpose(gradient_before_residual, ffn_input_weight),
            product_with_transpose(gradient_before_residual, ffn_input_up_weight),
        ),
        "mp",
    )
    gate_grad = gate_grad + per_expert(ffn_state["down"] * side_in)
    gradient_input_down = (spread_two * side_in).astype(brain_float)
    grad_in_down = contract_rows(ffn_state["normed"], gradient_input_down)
    logit_grad = softmax_backward(ffn_state["gates"], gate_grad).astype(brain_float)
    grad_route_two = contract_rows(ffn_state["normed"], logit_grad)
    grad_normed = (
        normed_sum
        + product_with_transpose(gradient_input_down, ffn_input_down_weight)
        + product_with_transpose(logit_grad, feedforward_router_weight)
    )
    grad_gain_two = jnp.sum(grad_normed * hidden_units_rows * ffn_state["scale"], 0)
    grad_hidden = gradient_output_rows.astype(single_precision) + norm_backward(
        hidden_units_rows,
        ffn_state["scale"],
        feedforward_norm_gain.astype(single_precision),
        grad_normed,
    )
    return (
        grad_hidden,
        (
            grad_ffout_up,
            gradient_ffn_output_down,
            grad_in_up,
            grad_in_down,
            grad_route_two,
            grad_gain_two,
        ),
    )


def attention_back(
    attention_saved,
    block_of_rows,
    grad_hidden,
    lengths,
    seq_count,
    seq_span,
    weight_collection,
    pos_bias,
    onehot,
):
    (
        attention_norm_gain,
        query_projection_weight,
        key_value_weight,
        attention_output_weight,
        down_joined,
        query_up_weight,
        key_value_up_weight,
        attention_output_down_rows,
        attention_output_up_weight,
        attention_router_weight,
    ) = weight_collection
    spread_one = attention_saved["spread"]
    rank_columns = spread_one.shape[1]
    row_count = block_of_rows.shape[0]
    gradient_branch_rows = grad_hidden.astype(brain_float)
    adapter_output_delta = product_with_transpose(gradient_branch_rows, attention_output_up_weight)
    grad_out_up = contract_rows(attention_saved["mixed_out"], gradient_branch_rows)
    gate_grad = per_expert(attention_saved["down_out"] * adapter_output_delta)
    grad_down_out = (spread_one * adapter_output_delta).astype(brain_float)
    gradient_attention_output_down = contract_rows(attention_saved["attended"], grad_down_out)
    grad_attended = (
        product_with_transpose(gradient_branch_rows, attention_output_weight)
        + product_with_transpose(grad_down_out, attention_output_down_rows)
    ).astype(brain_float)
    blocked = (seq_count, seq_span, -1, HEAD_WIDTH)
    grad_query_rows, grad_key_rows, grad_value_rows, bias_part = attend_backward(
        attention_saved["queries"].reshape(blocked),
        attention_saved["keys"].reshape(blocked),
        attention_saved["values"].reshape(blocked),
        pos_bias,
        lengths,
        seq_span,
        attention_saved["log_total"],
        grad_attended.reshape(blocked),
    )
    gradient_query_block = grad_query_rows.reshape(row_count, -1).astype(brain_float)
    gradient_key_block = grad_key_rows.reshape(row_count, -1).astype(brain_float)
    gradient_value_block = grad_value_rows.reshape(row_count, -1).astype(brain_float)
    blended_projection = attention_saved["mixed_qkv"]
    grad_query_up = contract_rows(blended_projection[:, :rank_columns], gradient_query_block)
    grad_keyval_up = jnp.stack(
        [
            contract_rows(
                blended_projection[:, rank_columns : 2 * rank_columns], gradient_key_block
            ),
            contract_rows(blended_projection[:, 2 * rank_columns :], gradient_value_block),
        ]
    )
    side_part = jnp.concatenate(
        [
            product_with_transpose(gradient_query_block, query_up_weight),
            product_with_transpose(gradient_key_block, key_value_up_weight[0]),
            product_with_transpose(gradient_value_block, key_value_up_weight[1]),
        ],
        1,
    )
    normed_part = (
        product_with_transpose(gradient_query_block, query_projection_weight)
        + product_with_transpose(gradient_key_block, key_value_weight[0])
        + product_with_transpose(gradient_value_block, key_value_weight[1])
    )
    normed_sum, side_qkv = (
        lax.psum(normed_part.astype(jnp.bfloat16), "mp").astype(jnp.float32),
        lax.psum(side_part.astype(jnp.bfloat16), "mp").astype(jnp.float32),
    )
    gate_grad = gate_grad + per_expert(attention_saved["down_qkv"] * side_qkv).reshape(
        row_count, 3, -1
    ).sum(1)
    grad_down_qkv = (jnp.tile(spread_one, (1, 3)) * side_qkv).astype(brain_float)
    grad_qkv_down = contract_rows(attention_saved["normed"], grad_down_qkv)
    grad_qkv_down = jnp.transpose(grad_qkv_down.reshape(-1, 3, rank_columns), (1, 0, 2))
    logit_grad = softmax_backward(attention_saved["gates"], gate_grad).astype(brain_float)
    grad_route_one = contract_rows(attention_saved["normed"], logit_grad)
    grad_normed = (
        normed_sum
        + product_with_transpose(grad_down_qkv, down_joined)
        + product_with_transpose(logit_grad, attention_router_weight)
    )
    grad_gain_one = jnp.sum(grad_normed * block_of_rows * attention_saved["scale"], 0)
    grad_rows = grad_hidden + norm_backward(
        block_of_rows,
        attention_saved["scale"],
        attention_norm_gain.astype(single_precision),
        grad_normed,
    )
    grad_table = table_grad(bias_part, seq_span, onehot)
    return (
        grad_rows,
        (
            grad_out_up,
            gradient_attention_output_down,
            grad_query_up,
            grad_keyval_up,
            grad_qkv_down,
            grad_route_one,
            grad_gain_one,
            grad_table,
        ),
    )


def reduce_grads(wide_local, data_local):
    grad_a_outrows, grad_a_ffrows = wide_local
    (
        grad_gain_one,
        grad_gain_two,
        grad_qkv_down,
        grad_query_up,
        grad_keyval_up,
        grad_out_up,
        grad_in_down,
        grad_in_up,
        grad_ffout_up,
        grad_route_one,
        grad_route_two,
        grad_table,
    ) = data_local
    wide_sums = lax.psum((grad_a_outrows, grad_a_ffrows), ("dp", "mp"))
    data_sums = lax.psum(
        (
            grad_gain_one,
            grad_gain_two,
            grad_qkv_down,
            grad_query_up,
            grad_keyval_up,
            grad_out_up,
            grad_in_down,
            grad_in_up,
            grad_ffout_up,
            grad_route_one,
            grad_route_two,
            grad_table,
        ),
        "dp",
    )
    return (wide_sums, data_sums)


def add_trees(left_op, right_op):
    return jax.tree.map(jnp.add, left_op, right_op)


def local(
    tokens,
    cotangent,
    attention_norm_gain,
    feedforward_norm_gain,
    query_projection_weight,
    key_value_weight,
    attention_output_weight,
    ffn_input_weight,
    ffn_output_weight,
    projection_down_weight,
    query_up_weight,
    key_value_up_weight,
    attention_output_down_weight,
    attention_output_up_weight,
    ffn_input_down_weight,
    ffn_input_up_weight,
    ffn_output_down_weight,
    ffn_output_up_weight,
    attention_router_weight,
    feedforward_router_weight,
    bucket_bias_table,
    offset_bucket_map,
    sequence_length_list,
):
    partition_index = lax.axis_index("mp")
    head_columns = query_projection_weight.shape[1]
    hidden_columns = ffn_input_weight.shape[1]
    short_rows = SHORT_SEQS * SHORT_LEN
    down_joined = jnp.concatenate(
        [projection_down_weight[0], projection_down_weight[1], projection_down_weight[2]], 1
    )
    onehot = (offset_bucket_map[:, None] == jnp.arange(BUCKETS, dtype=jnp.int32)[None, :]).astype(
        single_precision
    )
    query_all, keyval_all, out_all, in_all, ffout_all = (
        query_projection_weight,
        key_value_weight,
        attention_output_weight,
        ffn_input_weight,
        ffn_output_weight,
    )
    b_query_all, b_keyval_all, b_in_all, table_all = (
        query_up_weight,
        key_value_up_weight,
        ffn_input_up_weight,
        bucket_bias_table,
    )
    attention_output_down_rows = lax.dynamic_slice_in_dim(
        attention_output_down_weight, partition_index * head_columns, head_columns, 0
    )
    ffn_output_down_rows = lax.dynamic_slice_in_dim(
        ffn_output_down_weight, partition_index * hidden_columns, hidden_columns, 0
    )
    batches = (
        (0, SHORT_SEQS, SHORT_LEN, sequence_length_list[:SHORT_SEQS]),
        (short_rows, LONG_SEQS, LONG_LEN, sequence_length_list[SHORT_SEQS:]),
    )
    rel_bias = lax.dot(
        onehot,
        table_all.astype(single_precision),
        precision=highest,
        preferred_element_type=single_precision,
    )
    positions = jnp.arange(LONG_LEN, dtype=jnp.int32)
    offsets = positions[None, :] - positions[:, None] + LONG_LEN - 1
    pos_bias = jnp.transpose(jnp.take(rel_bias, offsets, axis=0), (2, 0, 1))
    attn_weights = (
        attention_norm_gain,
        query_all,
        keyval_all,
        out_all,
        down_joined,
        b_query_all,
        b_keyval_all,
        attention_output_down_rows,
        attention_output_up_weight,
        attention_router_weight,
    )
    ffn_weights = (
        feedforward_norm_gain,
        in_all,
        ffn_input_down_weight,
        b_in_all,
        feedforward_router_weight,
        ffout_all,
        ffn_output_down_rows,
        ffn_output_up_weight,
    )
    results = []
    stored = []
    for row_start, seq_count, seq_span, lengths in batches:
        block_of_rows = lax.dynamic_slice_in_dim(tokens, row_start, seq_count * seq_span, 0).astype(
            single_precision
        )
        attention_saved = attention_half(
            block_of_rows, lengths, seq_count, seq_span, attn_weights, pos_bias
        )
        ffn_state = ffn_local(attention_saved["hidden"], ffn_weights)
        feedforward_total, down_ff = lax.psum(
            (
                matrix_product(ffn_state["active"], ffout_all),
                matrix_product(ffn_state["active"], ffn_output_down_rows),
            ),
            "mp",
        )
        blended_feedforward = (ffn_state["spread"] * down_ff).astype(brain_float)
        results.append(
            (
                attention_saved["hidden"]
                + (feedforward_total + matrix_product(blended_feedforward, ffn_output_up_weight))
            ).astype(brain_float)
        )
        stored.append((None, None, down_ff))
    wide_total = None
    data_total = None
    input_grads = []
    for number, (row_start, seq_count, seq_span, lengths) in enumerate(batches):
        row_count = seq_count * seq_span
        block_of_rows = lax.dynamic_slice_in_dim(tokens, row_start, row_count, 0).astype(
            single_precision
        )
        gradient_output_rows = lax.dynamic_slice_in_dim(cotangent, row_start, row_count, 0)
        down_ff = stored[number][2]
        attention_saved = attention_half(
            block_of_rows, lengths, seq_count, seq_span, attn_weights, pos_bias
        )
        ffn_state = ffn_local(attention_saved["hidden"], ffn_weights)
        grad_hidden, ffn_grads = ffn_back(
            ffn_state, down_ff, attention_saved["hidden"], gradient_output_rows, ffn_weights
        )
        (
            grad_ffout_up,
            gradient_ffn_output_down,
            grad_in_up,
            grad_in_down,
            grad_route_two,
            grad_gain_two,
        ) = ffn_grads
        grad_rows, attn_grads = attention_back(
            attention_saved,
            block_of_rows,
            grad_hidden,
            lengths,
            seq_count,
            seq_span,
            attn_weights,
            pos_bias,
            onehot,
        )
        (
            grad_out_up,
            gradient_attention_output_down,
            grad_query_up,
            grad_keyval_up,
            grad_qkv_down,
            grad_route_one,
            grad_gain_one,
            grad_table,
        ) = attn_grads
        input_grads.append(grad_rows.astype(brain_float))
        wide_local = (
            lax.dynamic_update_slice_in_dim(
                jnp.zeros(attention_output_down_weight.shape, single_precision),
                gradient_attention_output_down,
                partition_index * head_columns,
                0,
            ),
            lax.dynamic_update_slice_in_dim(
                jnp.zeros(ffn_output_down_weight.shape, single_precision),
                gradient_ffn_output_down,
                partition_index * hidden_columns,
                0,
            ),
        )
        data_local = (
            grad_gain_one,
            grad_gain_two,
            grad_qkv_down,
            grad_query_up,
            grad_keyval_up,
            grad_out_up,
            grad_in_down,
            grad_in_up,
            grad_ffout_up,
            grad_route_one,
            grad_route_two,
            grad_table,
        )
        wide_local, data_local = reduce_grads(wide_local, data_local)
        if number == 0:
            wide_total, data_total = (wide_local, data_local)
        else:
            wide_total = add_trees(wide_total, wide_local)
            data_total = add_trees(data_total, data_local)
    output = jnp.concatenate(results, 0)
    grad_tokens = jnp.concatenate(input_grads, 0)
    grad_b_query = data_total[3]
    grad_b_keyval = data_total[4]
    grad_b_in = data_total[7]
    grad_bias = data_total[11]
    return (
        output,
        grad_tokens,
        data_total[0],
        data_total[1],
        data_total[2],
        grad_b_query,
        grad_b_keyval,
        wide_total[0],
        data_total[5],
        data_total[6],
        grad_b_in,
        wide_total[1],
        data_total[8],
        data_total[9],
        data_total[10],
        grad_bias,
    )


def solution(mesh):
    in_specs = (
        P("dp", None),
        P("dp", None),
        P(),
        P(),
        P(None, "mp"),
        P(None, None, "mp"),
        P("mp", None),
        P(None, "mp"),
        P("mp", None),
        P(),
        P(None, "mp"),
        P(None, None, "mp"),
        P(),
        P(),
        P(),
        P(None, "mp"),
        P(),
        P(),
        P(),
        P(),
        P(None, "mp"),
        P(),
        P("dp"),
    )
    out_specs = (
        P("dp", None),
        P("dp", None),
        P(),
        P(),
        P(),
        P(None, "mp"),
        P(None, None, "mp"),
        P(),
        P(),
        P(),
        P(None, "mp"),
        P(),
        P(),
        P(),
        P(),
        P(None, "mp"),
    )
    return jax.shard_map(local, mesh=mesh, in_specs=in_specs, out_specs=out_specs, check_vma=False)
```

profile of v0, /device:TPU:0, one launch (start us, length us, event | category | flops | bytes accessed | tf_op | source)
XLA Modules:
  0.0 2463.6 jit_solution(15036460114068557640)
XLA Ops:
  49.9 861.5 %gather_fusion = f32[262144,3]{1,0:T(8,128)} fusion(f32[1023,3]{1,0:T(8,128)S(1)} %fusion.131, s32[262144]{0:T(1024)S(1)} %broadcast_clamp_fusion), kind=kCustom, calls=%fused_computation | custom fusion | bytes 7340032 | tf_op jit(solution)/shard_map/jit(_take)/gather | solution.py:538
  911.5 71.5 %copy.136 = f32[512,512,3]{0,1,2:T(8,128)} copy(f32[512,512,3]{2,1,0:T(8,128)} %bitcast.8) | data formatting | bytes 6291456 | tf_op jit(solution)/shard_map/jit(_take)/gather | solution.py:538
  1031.0 7.4 fusion.39
  1043.1 222.4 %all-reduce.23.cloned.1.call-done = (f32[2048,768]{1,0:T(8,128)}, f32[2048,40]{0,1:T(8,128)}, f32[2048,768]{1,0:T(8,128)}, f32[2048,40]{0,1:T(8,128)}) async-done(((f32[2048,768]{1,0:T(8,128)}, f32[2048,40]{0,1:T(8,128)}, f32[2048,768]{1,0:T(8,128)}, f32[2048,40]{0,1:T(8,128)}), (f32[2048,768]{1,0:T(8,128)}, f32[2048,40]{0,1:T(8,128)}, f32[2048,768]{1,0:T(8,128)}, ...) | async-done | bytes 13238288 | tf_op jit(solution)/shard_map/psum | solution.py:189
  1273.4 5.5 multiply_reduce_fusion.5
  1299.2 5.6 multiply_convert_fusion.3
  1355.2 438.8 %all-reduce.21.cloned.1.call-done = (f32[2048,768]{1,0:T(8,128)}, f32[2048,40]{0,1:T(8,128)}, f32[2048,768]{1,0:T(8,128)}, f32[2048,40]{0,1:T(8,128)}, f32[2048,...) async-done(((f32[2048,768]{1,0:T(8,128)}, f32[2048,40]{0,1:T(8,128)}, f32[2048,768]{1,0:T(8,128)}, f32[2048,40]{0,1:T(8,128)}, ...) | async-done | bytes 26476560 | tf_op jit(solution)/shard_map/psum | solution.py:571
  1811.2 6.7 add_add_fusion.1
  1817.9 10.4 multiply_reduce_fusion.2
  1828.4 11.5 subtract_add_fusion.1
  1845.3 7.3 fusion.51
  1852.7 11.0 multiply_reduce_fusion
  1863.7 10.1 convert_reduce_fusion
  1921.3 26.0 %rev.7 = f32[3,512,512]{1,2,0:T(8,128)} reverse(f32[3,512,512]{1,2,0:T(8,128)} %get-tuple-element.58), dimensions={1} | reverse | bytes 6291456 | tf_op jit(solution)/shard_map/rev | solution.py:130
  1956.2 7.1 copy.194
  1967.9 13.1 reshape.348
  1987.9 7.8 add_convert_fusion
  1995.9 5.7 add_convert_fusion.2
  2041.0 100.6 %all-reduce.25.cloned.1.call-done = (bf16[2048,120]{0,1:T(8,128)(2,1)}, bf16[2048,768]{1,0:T(8,128)(2,1)}, bf16[2048,120]{0,1:T(8,128)(2,1)}, bf16[2048,768]{1,0:T(8,128)(2,1)}) async-done(((bf16[2048,120]{0,1:T(8,128)(2,1)}, bf16[2048,768]{1,0:T(8,128)(2,1)}, bf16[2048,120]{0,1:T(8,128)(2,1)}, bf16[2048,768]{1,0:T(8,128)(2,1)}), (bf16[2048,120]{0,1:T(8,128)(2,1)}, bf16[2048,768]{1,0:T(8,128)(2,1)}, ...) | async-done | bytes 7274512 | tf_op jit(solution)/shard_map/psum | solution.py:393
  2164.0 8.1 fusion.21
  2175.8 11.8 fusion.17
  2190.7 85.5 %all-reduce.15.cloned.1.call-done = (f32[768,40]{0,1:T(8,128)}, f32[3072,40]{0,1:T(8,128)}) async-done(((f32[768,40]{0,1:T(8,128)}, f32[3072,40]{0,1:T(8,128)}), (f32[768,40]{0,1:T(8,128)}, f32[3072,40]{0,1:T(8,128)})) %all-reduce.15.cloned.1.call-update) | async-done | bytes 614416 | tf_op jit(solution)/shard_map/psum | solution.py:447
  2276.3 77.9 %all-reduce.17.cloned.1.call-done = (f32[768]{0:T(1024)}, f32[768]{0:T(1024)}, f32[40,192]{1,0:T(8,128)}, f32[2,40,192]{2,1,0:T(8,128)}, f32[768,10]{0,1:T(8,128)}, /*index=5*/f32[768,10]{0,1:T(8,128)}, f32[32,3]{0,1:T(4,128)}) async-done(((f32[768]{0:T(1024)}, f32[768]{0:T(1024)}, f32[40,192]{1,0:T(8,128)}, f32[2,40,192]{2,1,0:T(8,128)}, f32[768,10]{0,1:T(8,128)}, /*index=5*/f32[768,10]{0,1:T(8,128)}, ...) | async-done | bytes 160144 | tf_op jit(solution)/shard_map/psum | solution.py:448
  2354.1 81.5 %all-reduce.19.cloned.1.call-done = (f32[3,768,40]{1,2,0:T(8,128)}, f32[40,768]{1,0:T(8,128)}, f32[768,40]{0,1:T(8,128)}, f32[40,768]{1,0:T(8,128)}, f32[40,768]{1,0:T(8,128)}) async-done(((f32[3,768,40]{1,2,0:T(8,128)}, f32[40,768]{1,0:T(8,128)}, f32[768,40]{0,1:T(8,128)}, f32[40,768]{1,0:T(8,128)}, f32[40,768]{1,0:T(8,128)}), (f32[3,768,40]{1,2,0:T(8,128)}, f32[40,768]{1,0:T(8,128)}, f32[768,40]{0,1:T(8,128)}, ...) | async-done | bytes 860176 | tf_op jit(solution)/shard_map/psum | solution.py:448
  (693 shorter events, 351.5 us)
Async XLA Ops:
  7.2 1023.8 %copy-start = (bf16[768,768]{1,0:T(8,128)(2,1)S(1)}, bf16[768,768]{1,0:T(8,128)(2,1)}, u32[]{:S(2)}) copy-start(bf16[768,768]{1,0:T(8,128)(2,1)} %param.31) | copy-start | bytes 3538948
  7.2 1258.3 %all-reduce.23.cloned.1.call-start = ((), (), s32[]{:S(2)}) async-start(), calls=%async_computation.4 | async-start | bytes 26476544 | tf_op jit(solution)/shard_map/psum | solution.py:189
  911.5 71.5 %copy-start.179 = (s32[20]{0:T(128)S(1)}, s32[20]{0:T(128)}, u32[]{:S(2)}) copy-start(s32[20]{0:T(128)} %param.45) | copy-start | bytes 244
  911.5 71.6 %copy-start.35 = (f32[2048,192]{0,1:T(8,128)S(1)}, f32[2048,192]{0,1:T(8,128)}, u32[]{:S(2)}) copy-start(f32[2048,192]{0,1:T(8,128)} %fusion.143) | copy-start | bytes 4718596
  911.5 71.6 %copy-start.43 = (bf16[2,768,192]{1,2,0:T(8,128)(2,1)S(1)}, bf16[2,768,192]{1,2,0:T(8,128)(2,1)}, u32[]{:S(2)}) copy-start(bf16[2,768,192]{1,2,0:T(8,128)(2,1)} %param.28) | copy-start | bytes 1769476
  983.1 21.0 copy-start.104
  1009.3 19.0 copy-start.30
  1030.3 763.6 %all-reduce.21.cloned.1.call-start = ((), (), s32[]{:S(2)}) async-start(), calls=%async_computation.3 | async-start | bytes 52953088 | tf_op jit(solution)/shard_map/psum | solution.py:571
  1031.0 247.9 %copy-start.165 = (f32[768]{0:T(1024)}, f32[768]{0:T(1024)S(1)}, u32[]{:S(2)}) copy-start(f32[768]{0:T(1024)S(1)} %convert_element_type.330) | copy-start | bytes 9220
  1038.4 229.5 %copy-start.102 = (bf16[40,768]{1,0:T(8,128)(2,1)S(1)}, bf16[40,768]{1,0:T(8,128)(2,1)}, u32[]{:S(2)}) copy-start(bf16[40,768]{1,0:T(8,128)(2,1)} %param.36) | copy-start | bytes 184324
  1313.2 22.3 copy-start.110
  1344.6 796.9 %all-reduce.25.cloned.1.call-start = ((), (), s32[]{:S(2)}) async-start(), calls=%async_computation.5 | async-start | bytes 14548992 | tf_op jit(solution)/shard_map/psum | solution.py:393
  1349.2 447.5 %copy-start.95 = (bf16[768,40]{0,1:T(8,128)(2,1)S(1)}, bf16[768,40]{0,1:T(8,128)(2,1)}, u32[]{:S(2)}) copy-start(bf16[768,40]{0,1:T(8,128)(2,1)} %param.37) | copy-start | bytes 184324
  2005.1 21.4 slice-start.13
  2005.2 271.1 %all-reduce.15.cloned.1.call-start = ((), (), s32[]{:S(2)}) async-start(), calls=%async_computation | async-start | bytes 1228800 | tf_op jit(solution)/shard_map/psum | solution.py:447
  2037.0 104.5 %copy-start.51 = (f32[2048,40]{0,1:T(8,128)S(1)}, f32[2048,40]{0,1:T(8,128)}, u32[]{:S(2)}) copy-start(f32[2048,40]{0,1:T(8,128)} %tile.12) | copy-start | bytes 983044
  2037.0 104.5 %copy-start.71 = (f32[2048,120]{0,1:T(8,128)S(1)}, f32[2048,120]{0,1:T(8,128)}, u32[]{:S(2)}) copy-start(f32[2048,120]{0,1:T(8,128)} %get-tuple-element.112) | copy-start | bytes 2949124
  2040.2 108.1 %copy-start.69 = (f32[2048,10]{0,1:T(8,128)S(1)}, f32[2048,10]{0,1:T(8,128)}, u32[]{:S(2)}) copy-start(f32[2048,10]{0,1:T(8,128)} %copy-done.68) | copy-start | bytes 245764
  2040.2 108.1 %copy-start.122 = (f32[2048,10]{0,1:T(8,128)S(1)}, f32[2048,10]{0,1:T(8,128)}, u32[]{:S(2)}) copy-start(f32[2048,10]{0,1:T(8,128)} %reduce_sum.397) | copy-start | bytes 245764
  2040.2 108.1 %copy-start.139 = (f32[2048]{0:T(1024)S(1)}, f32[2048]{0:T(1024)}, u32[]{:S(2)}) copy-start(f32[2048]{0:T(1024)} %copy-done.138) | copy-start | bytes 24580
  2040.2 108.1 %copy-start.155 = (f32[2048]{0:T(1024)S(1)}, f32[2048]{0:T(1024)}, u32[]{:S(2)}) copy-start(f32[2048]{0:T(1024)} %copy-done.154) | copy-start | bytes 24580
  2040.2 108.3 %copy-start.128 = (bf16[768,10]{0,1:T(8,128)(2,1)S(1)}, bf16[768,10]{0,1:T(8,128)(2,1)}, u32[]{:S(2)}) copy-start(bf16[768,10]{0,1:T(8,128)(2,1)} %param.41) | copy-start | bytes 46084
  2040.2 313.9 %all-reduce.17.cloned.1.call-start = ((), (), s32[]{:S(2)}) async-start(), calls=%async_computation.1 | async-start | bytes 462848 | tf_op jit(solution)/shard_map/psum | solution.py:448
  2175.3 260.4 %all-reduce.19.cloned.1.call-start = ((), (), s32[]{:S(2)}) async-start(), calls=%async_computation.2 | async-start | bytes 1720320 | tf_op jit(solution)/shard_map/psum | solution.py:448
  (197 other events, 1157.2 us)
Sparse Core Ops, SparseCore 0:
  1030.5 235.0 all-reduce.22
  1344.7 449.2 all-reduce.20
  2005.3 136.2 all-reduce.24
  2148.1 128.1 all-reduce.14
  2281.5 72.5 all-reduce.16
  2359.7 75.9 all-reduce.18
where the time goes:
time: 2480 us; the launch traced here: 2460 us
  local copies, waits for them, and re-layouts  1060 us (43%)
  waiting for transfers between devices  1010 us (41%)
  matrix products  294 us (12%)
  other arithmetic  86.4 us (3%)
    gather x2, local copies, waits for them, and re-layouts, local(): pos_bias = jnp.transpose(jnp.take(rel_bias, offsets, axis=0), (2, 0, 1))  933 us
    psum x1, waiting for transfers between devices, local(): lax.psum((matrix_product(ffn_state['active'], ffout_all), matrix_product(...  439 us
    psum x1, waiting for transfers between devices, attention_half(): lax.psum((matrix_product(attended_rows, attention_output_weight), matrix_...  222 us
    psum x2, waiting for transfers between devices, reduce_grads(): lax.psum((grad_gain_one, grad_gain_two, grad_qkv_down, grad_query_up, gra...  159 us
    dot_general x36, matrix products, product_with_transpose(): lax.dot_general(left_op, right_op, (((1,), (1,)), ((), ())), preferred_el...  120 us
    psum x1, waiting for transfers between devices, attention_back(): lax.psum(side_part.astype(jnp.bfloat16), 'mp').astype(jnp.float32)  101 us
    dot_general x36, matrix products, matrix_product(): return jnp.dot(left_op, right_op, preferred_element_type=single_precision)  98.1 us
    psum x1, waiting for transfers between devices, reduce_grads(): wide_sums = lax.psum((grad_a_outrows, grad_a_ffrows), ('dp', 'mp'))  85.5 us
  transfers between devices with their start and end apart: 6, of which 6 were waited for; matrix products, arithmetic and copies ran while one was open for 4% of the time, Pallas kernels for 0%

commit v1 on v0

v1 whole, which is shorter than its diff:
```python
import functools

import jax
import jax.numpy as jnp
import numpy as np
from jax import lax
from jax.experimental import pallas as pl
from jax.experimental.pallas import tpu as pltpu
from jax.sharding import PartitionSpec as P

HEAD_WIDTH = 64
BUCKETS = 32
ADAPTER_RANK = 4
SHORT_LEN = 128
LONG_LEN = 512
LONG_SEQS = 4
SHORT_SEQS = 16
MODEL_WIDTH = 768
LORA = 40
EXPERTS = 10
LANES = 128
HALF_ROWS = 512
ROWS = 1024
EPS = 1e-06
NEG = -1e9

bf16 = jnp.bfloat16
f32 = jnp.float32
VMEM_LIMIT = 56 * 1024 * 1024


def nn(a, b):
    return jnp.dot(a, b, preferred_element_type=f32)


def nt(a, b):
    return lax.dot_general(a, b, (((1,), (1,)), ((), ())), preferred_element_type=f32)


def tn(a, b):
    return lax.dot_general(a, b, (((0,), (0,)), ((), ())), preferred_element_type=f32)


def lane_index(shape):
    return lax.broadcasted_iota(jnp.int32, shape, 1)


def softmax_repeated(logits, valid, repeats):
    logits = jnp.where(lane_index(logits.shape) < valid, logits, -1e30)
    raised = jnp.exp(logits - jnp.max(logits, -1, keepdims=True))
    return raised * (repeats / jnp.sum(raised, -1, keepdims=True))


def logit_gradient(products, gates, group, pick):
    high = products.astype(bf16)
    low = (products - high.astype(f32)).astype(bf16)
    gate_grad = nn(high, group) + nn(low, group)
    inner = jnp.sum(gates * gate_grad, -1, keepdims=True) * (1.0 / ADAPTER_RANK)
    logit_grad = (gates * (gate_grad - inner)).astype(bf16)
    return nn(logit_grad, pick).astype(bf16)


PACK_ROWS = 864


def pack_kernel(q_ref, kv_ref, wo_ref, qup_ref, kvup_ref, table_ref, up_ref, pack_ref):
    pack_ref[0:192, :] = q_ref[...]
    pack_ref[192:384, :] = kv_ref[0]
    pack_ref[384:576, :] = kv_ref[1]
    pack_ref[576:768, :] = wo_ref[...]
    ups = jnp.concatenate([qup_ref[...], kvup_ref[0], kvup_ref[1], jnp.zeros((LORA, 192), bf16)], 1).astype(f32)
    table = jnp.pad(table_ref[...].astype(f32), ((0, 5), (0, MODEL_WIDTH - BUCKETS)))
    pack_ref[768:816, :] = jnp.concatenate([ups, table], 0).astype(bf16)
    pack_ref[816:864, :] = jnp.pad(up_ref[...].astype(f32), ((0, 8), (0, 0))).astype(bf16)


def pad_to(rows, count):
    if rows.shape[0] == count:
        return rows
    return jnp.concatenate([rows, jnp.zeros((count - rows.shape[0], rows.shape[1]), rows.dtype)], 0)


def repeated_router(router, copies):
    rows = lax.broadcasted_iota(jnp.int32, (LANES, EXPERTS), 0)
    first = ADAPTER_RANK * lax.broadcasted_iota(jnp.int32, (LANES, EXPERTS), 1)
    hot = jnp.zeros((LANES, EXPERTS), jnp.bool_)
    for c in range(copies):
        hot = hot | ((rows >= LORA * c + first) & (rows < LORA * c + first + ADAPTER_RANK))
    return nn(hot.astype(bf16), router).astype(bf16)


def down_rows(downs, router_rows):
    downs = pad_to(jnp.concatenate([part.astype(f32) for part in downs], 0), LANES)
    return jnp.concatenate([downs, pad_to(router_rows.astype(f32), LANES)], 0).astype(bf16)


def join_packs(one_ref, two_ref, ups_one, ups_two, joined_ref, ups_ref):
    ups = []
    for part in range(3):
        joined_ref[384 * part : 384 * part + 192, :] = one_ref[192 * part : 192 * part + 192, :]
        joined_ref[384 * part + 192 : 384 * part + 384, :] = two_ref[192 * part : 192 * part + 192, :]
        cols = slice(192 * part, 192 * part + 192)
        piece = jnp.concatenate([ups_one[:LORA, cols], ups_two[:LORA, cols]], 1).astype(f32)
        zero = jnp.zeros((LORA, 384), f32)
        ups.append(jnp.concatenate([piece if p == part else zero for p in range(3)], 1))
    ups_ref[...] = pad_to(jnp.concatenate(ups, 0), LANES).astype(bf16)


def project(normed, mixed, joined_ref, ups_ref, q_ref, k_ref, v_ref):
    result = nt(normed, joined_ref[...]) + nn(mixed, ups_ref[...])
    result = result.astype(bf16)
    q_ref[...] = result[:, :384]
    k_ref[...] = result[:, 384:768]
    v_ref[...] = result[:, 768:]


def first_kernel(
    place, x_ref, gain_ref, downs_in, router_ref, one_ref, ups_one, two_ref, ups_two,
    normed_ref, mixed_ref, spread_ref, downs_ref, q_ref, k_ref, v_ref, joined_ref, ups_ref, down_scr,
):
    @pl.when(pl.program_id(0) == 0)
    def _():
        join_packs(one_ref, two_ref, ups_one, ups_two, joined_ref, ups_ref)
        down_scr[...] = down_rows([downs_in[0], downs_in[1], downs_in[2]], repeated_router(router_ref[...], 3))

    x = x_ref[...].astype(f32)
    scale = lax.rsqrt(jnp.mean(x * x, -1, keepdims=True) + EPS)
    normed = (x * scale * gain_ref[...].astype(f32)).astype(bf16)
    normed_ref[...] = normed
    both = nt(normed, down_scr[...])
    downs = both[:, :LANES]
    spread = softmax_repeated(both[:, LANES:], 3 * LORA, 3.0 * ADAPTER_RANK)
    mixed = (spread * downs).astype(bf16)
    mixed_ref[...] = mixed
    spread_ref[...] = spread
    downs_ref[...] = downs
    project(normed, mixed, joined_ref, ups_ref, q_ref, k_ref, v_ref)


def second_kernel(
    normed_ref, mixed_ref, one_ref, ups_one, two_ref, ups_two, q_ref, k_ref, v_ref, joined_ref, ups_ref
):
    @pl.when(pl.program_id(0) == 0)
    def _():
        join_packs(one_ref, two_ref, ups_one, ups_two, joined_ref, ups_ref)

    project(normed_ref[...], mixed_ref[...], joined_ref, ups_ref, q_ref, k_ref, v_ref)


def split_pair(rows):
    lanes = lane_index(rows.shape)
    zero = jnp.zeros_like(rows)
    return jnp.concatenate([jnp.where(lanes < HEAD_WIDTH, rows, zero), jnp.where(lanes < HEAD_WIDTH, zero, rows)], 0)


def merge_pair(turned):
    return jnp.concatenate([turned[:HEAD_WIDTH, :LANES], turned[HEAD_WIDTH:, LANES:]], 0).T


def bucket_hot(map_ref):
    rows = lax.broadcasted_iota(jnp.int32, (BUCKETS, 2 * LONG_LEN), 0)
    return rows == map_ref[...]


def build_tiles(one_ref, two_ref, map_ref, tile_ref):
    pair = pl.program_id(0)
    hot = bucket_hot(map_ref).astype(bf16)
    table = jnp.concatenate(
        [one_ref[LORA : LORA + 8, :BUCKETS].astype(f32), two_ref[LORA : LORA + 8, :BUCKETS].astype(f32)], 0
    )
    by_offset = nn(table.astype(bf16), hot)
    heads = lax.broadcasted_iota(jnp.int32, (16, 1), 0)
    heads = jnp.where(heads < 8, heads, heads - 5)
    used = lax.broadcasted_iota(jnp.int32, (16, 1), 0)
    heads = jnp.where((used < 3) | ((used >= 8) & (used < 11)), heads, -1)
    rows_in = lax.broadcasted_iota(jnp.int32, (LANES, LANES), 0)
    lanes = lane_index((LANES, LANES))
    for t in range(2):
        row = jnp.sum(jnp.where(heads == 2 * pair + t, by_offset, 0.0), 0, keepdims=True)
        for d in range(7):
            block = 6 - d
            low = jnp.broadcast_to(row[:, LANES * block : LANES * block + LANES], (LANES, LANES))
            high = jnp.broadcast_to(row[:, LANES * block + LANES : LANES * block + 2 * LANES], (LANES, LANES))
            low = pltpu.roll(low, 1, 1, stride=1, stride_axis=0)
            high = pltpu.roll(high, 1, 1, stride=1, stride_axis=0)
            tile_ref[d, :, LANES * t : LANES * t + LANES] = jnp.where(lanes <= rows_in, low, high).astype(bf16)


def chunk_scores(keys, pair_queries, tiles, length):
    scores = nt(keys, pair_queries) + tiles
    positions = lax.broadcasted_iota(jnp.int32, scores.shape, 0)
    return jnp.where(positions < length, scores, NEG)


def chunk_layout():
    chunks = []
    for c in range(LONG_LEN // LANES):
        chunks.append((HALF_ROWS, LONG_LEN, HALF_ROWS + LANES * c, 3 - c, 4))
    for s in range(HALF_ROWS // SHORT_LEN):
        chunks.append((LANES * s, SHORT_LEN, LANES * s, 3, s))
    return chunks


def length_of(place, lengths, which):
    m = place[0]
    if which == 4:
        return lengths[SHORT_SEQS + m]
    return lengths[4 * m + which]


def tiles_of(tile_ref, first, span):
    return jnp.concatenate([tile_ref[first + b].astype(f32) for b in range(span // LANES)], 0)


def forward_attention(place, lengths, q_ref, k_ref, v_ref, one_ref, two_ref, map_ref, o_ref, lse_ref, tile_ref):
    tiles = tile_ref.at[0]
    build_tiles(one_ref, two_ref, map_ref, tiles)
    for number, (key_row, span, query_row, first, which) in enumerate(chunk_layout()):
        keys = k_ref[key_row : key_row + span, :]
        values_turned = v_ref[key_row : key_row + span, :].T
        queries = split_pair(q_ref[query_row : query_row + LANES, :])
        scores = chunk_scores(keys, queries, tiles_of(tiles, first, span), length_of(place, lengths, which))
        peak = jnp.max(scores, 0, keepdims=True)
        raised = jnp.exp(scores - peak)
        total = jnp.sum(raised, 0, keepdims=True)
        lse_ref[0, number : number + 1, :] = peak + jnp.log(total)
        weights = (raised * (1.0 / total)).astype(bf16)
        o_ref[query_row : query_row + LANES, :] = merge_pair(nn(values_turned, weights)).astype(bf16)


def backward_attention(
    place, lengths, q_ref, k_ref, v_ref, do_ref, lse_ref, tile_ref, map_ref, turn_ref,
    dq_ref, dk_ref, dv_ref, table_ref, weights_all, grads_all, queries_all, douts_all, diagonal,
):
    diagonal[...] = jnp.zeros_like(diagonal)
    turn = turn_ref[...]
    for number, (key_row, span, query_row, first, which) in enumerate(chunk_layout()):
        long = which == 4
        keys = k_ref[key_row : key_row + span, :]
        values = v_ref[key_row : key_row + span, :]
        queries = split_pair(q_ref[query_row : query_row + LANES, :])
        douts = split_pair(do_ref[query_row : query_row + LANES, :])
        scores = chunk_scores(keys, queries, tiles_of(tile_ref.at[0], first, span), length_of(place, lengths, which))
        probs = jnp.exp(scores - lse_ref[0, number : number + 1, :])
        weights = probs.astype(bf16)
        grad_probs = nt(values, douts)
        inner = jnp.sum(probs * grad_probs, 0, keepdims=True)
        grads = (probs * (grad_probs - inner)).astype(bf16)
        dq_ref[query_row : query_row + LANES, :] = merge_pair(nn(keys.T, grads)).astype(bf16)
        for b in range(span // LANES):
            diagonal[first + b] += nn(turn, grads[LANES * b : LANES * b + LANES, :])
        if long:
            at = 2 * LANES * number
            weights_all[:, at : at + 2 * LANES] = weights
            grads_all[:, at : at + 2 * LANES] = grads
            queries_all[at : at + 2 * LANES, :] = queries
            douts_all[at : at + 2 * LANES, :] = douts
        else:
            dv_ref[key_row : key_row + span, :] = nn(weights, douts).astype(bf16)
            dk_ref[key_row : key_row + span, :] = nn(grads, queries).astype(bf16)
    dv_ref[HALF_ROWS:, :] = nn(weights_all[...], douts_all[...]).astype(bf16)
    dk_ref[HALF_ROWS:, :] = nn(grads_all[...], queries_all[...]).astype(bf16)
    rows_in = lax.broadcasted_iota(jnp.int32, (LANES, LANES), 0)
    lanes = lane_index((LANES, LANES))
    hot = bucket_hot(map_ref).astype(f32)
    sums = []
    for t in range(2):
        pieces = [jnp.zeros((1, LANES), f32) for _ in range(8)]
        for d in range(7):
            block = 6 - d
            rolled = pltpu.roll(diagonal[d, :, LANES * t : LANES * t + LANES], 0, 1, stride=1, stride_axis=0)
            low = jnp.where(lanes >= rows_in, rolled, 0.0)
            pieces[block] = pieces[block] + jnp.sum(low, 0, keepdims=True)
            pieces[block + 1] = pieces[block + 1] + jnp.sum(rolled - low, 0, keepdims=True)
        sums.append(jnp.concatenate(pieces, 1))
    sums = jnp.concatenate(sums + [jnp.zeros((6, 2 * LONG_LEN), f32)], 0)
    table = lax.dot_general(
        sums, hot, (((1,), (1,)), ((), ())), precision=lax.Precision.HIGHEST, preferred_element_type=f32
    )
    table_ref[0] = jnp.concatenate([table, jnp.zeros((8, LANES - BUCKETS), f32)], 1)


def feedforward_shard(normed, cot, mixed, grad_down, win_ref, up, wout_ref, low):
    before = nn(normed, win_ref[...]) + nn(mixed, up)
    sig = jax.nn.sigmoid(before)
    active = (before * sig).astype(bf16)
    out = nn(active, wout_ref[...])
    down = nt(active, low)
    grad_active = (nt(cot, wout_ref[...]) + nn(grad_down, low)).astype(bf16).astype(f32)
    grad_before = (sig * (1.0 + before * (1.0 - sig)) * grad_active).astype(bf16)
    back = nt(grad_before, win_ref[...])
    side = nt(grad_before, up)
    grad_up = tn(mixed, grad_before)[:LORA]
    grad_low = tn(grad_down, active)[:LORA]
    return out, down, back, side, grad_up, grad_low


def fill_output_maps(place, ao_in, bo_in, wos, ao_scr, bo_scr, wo_scr):
    for j, wo in enumerate(wos):
        wo_scr[192 * j : 192 * j + 192, :] = wo[...]
    bo_scr[...] = pad_to(bo_in[...].astype(f32), LANES).astype(bf16)
    for at in range(4):

        @pl.when(place[0] == at)
        def _():
            pieces = [ao_in[:, 192 * (at ^ j) : 192 * (at ^ j) + 192] for j in range(4)]
            ao_scr[...] = pad_to(jnp.concatenate(pieces, 1).astype(f32), LANES).astype(bf16)


def fill_padded(scr, sources):
    for j, source in enumerate(sources):
        scr[j] = pad_to(source[:LORA, :].astype(f32), LANES).astype(bf16)


def middle_kernel(
    place, x_ref, cot_ref, aa_ref, ab_ref, wo0, wo1, wo2, wo3, ao_in, bo_in, spread1_ref, gain_ref,
    down_in, router_ref, bf_in, win0, up0, wout0, low0, win1, up1, wout1, low1,
    hidden_ref, normed_ref, spread_ref, gdown_ref, mixed_ref, downi_ref, sidef_ref, downo_ref, mixo_ref,
    out_ref, down_ref, back_ref, side_ref, shard_ref,
    ao_scr, bo_scr, wo_scr, down_scr, bf_scr, up_scr, low_scr,
):
    first = pl.program_id(0) == 0

    @pl.when(first)
    def _():
        fill_output_maps(place, ao_in, bo_in, (wo0, wo1, wo2, wo3), ao_scr, bo_scr, wo_scr)
        down_scr[...] = down_rows([down_in[...]], repeated_router(router_ref[...], 1))
        bf_scr[...] = pad_to(bf_in[...].astype(f32), LANES).astype(bf16)
        fill_padded(up_scr, (up0, up1))
        fill_padded(low_scr, (low0, low1))
        shard_ref[...] = jnp.zeros_like(shard_ref)

    attended = jnp.concatenate([aa_ref[...], ab_ref[...]], 1)
    downo = nt(attended, ao_scr[...])
    mixo = (spread1_ref[...] * downo).astype(bf16)
    hidden = x_ref[...].astype(f32) + (nn(attended, wo_scr[...]) + nn(mixo, bo_scr[...]))
    downo_ref[...] = downo
    mixo_ref[...] = mixo
    hidden_ref[...] = hidden
    scale = lax.rsqrt(jnp.mean(hidden * hidden, -1, keepdims=True) + EPS)
    normed = (hidden * scale * gain_ref[...].astype(f32)).astype(bf16)
    normed_ref[...] = normed
    both = nt(normed, down_scr[...])
    downi = both[:, :LANES]
    spread = softmax_repeated(both[:, LANES:], LORA, 1.0 * ADAPTER_RANK)
    mixed = (spread * downi).astype(bf16)
    cot = cot_ref[...]
    sidef = nt(cot, bf_scr[...])
    gdown = (spread * sidef).astype(bf16)
    spread_ref[...] = spread
    downi_ref[...] = downi
    mixed_ref[...] = mixed
    sidef_ref[...] = sidef
    gdown_ref[...] = gdown
    for j, (win, wout) in enumerate(((win0, wout0), (win1, wout1))):
        out, down, back, side, grad_up, grad_low = feedforward_shard(
            normed, cot, mixed, gdown, win, up_scr[j], wout, low_scr[j]
        )
        if j == 0:
            out_ref[...] = out
            down_ref[...] = down
            back_ref[...] = back
            side_ref[...] = side
        else:
            out_ref[...] += out
            down_ref[...] += down
            back_ref[...] += back
            side_ref[...] += side
        shard_ref[j, 0] += grad_up
        shard_ref[j, 1] += grad_low


def send_pieces(pieces, own_ref, sent_refs):
    own_ref[...] = pieces[0]
    for j, sent in enumerate(sent_refs):
        sent[...] = pieces[j + 1].astype(bf16)


def post_kernel(
    place, cot_ref, aa_ref, ab_ref, wo0, wo1, wo2, wo3, ao_in, bo_in, spread1_ref, gain_ref,
    down_in, router_ref, bf_in, win0, up0, wout0, low0, win1, up1, wout1, low1, group_ref, pick_ref,
    hidden_ref, normed_ref, spread_ref, gdown_ref, mixed_ref, downi_ref, sidef_ref, downo_ref, mixo_ref,
    out_ref, down_ref, back_ref, side_ref, shard_ref,
    result_ref, ghidden_ref, ga_ref, gb_ref, prod_ref, ao_grad, own_ref, sent1, sent2, sent3,
    ao_scr, bo_scr, wo_scr, down_scr, bf_scr, up_scr, low_scr,
    shard_acc, pair_acc, bff_acc, bo_acc, ao_acc, gain_acc, pieces,
):
    step = pl.program_id(0)

    @pl.when(step == 0)
    def _():
        fill_output_maps(place, ao_in, bo_in, (wo0, wo1, wo2, wo3), ao_scr, bo_scr, wo_scr)
        down_scr[...] = down_rows([down_in[...]], router_ref[...])
        bf_scr[...] = pad_to(bf_in[...].astype(f32), LANES).astype(bf16)
        fill_padded(up_scr, (up0, up1))
        fill_padded(low_scr, (low0, low1))
        shard_acc[...] = jnp.zeros_like(shard_acc)
        pair_acc[...] = jnp.zeros_like(pair_acc)
        bff_acc[...] = jnp.zeros_like(bff_acc)
        bo_acc[...] = jnp.zeros_like(bo_acc)
        ao_acc[...] = jnp.zeros_like(ao_acc)
        gain_acc[...] = jnp.zeros_like(gain_acc)

    normed, cot, mixed, gdown = normed_ref[...], cot_ref[...], mixed_ref[...], gdown_ref[...]
    total, downf, back, sidei = out_ref[...], down_ref[...], back_ref[...], side_ref[...]
    for j, (win, wout) in enumerate(((win0, wout0), (win1, wout1))):
        out, down, more, side, grad_up, grad_low = feedforward_shard(
            normed, cot, mixed, gdown, win, up_scr[j], wout, low_scr[j]
        )
        total = total + out
        downf = downf + down
        back = back + more
        sidei = sidei + side
        shard_acc[j, 0] += grad_up
        shard_acc[j, 1] += grad_low
    spread = spread_ref[...]
    hidden = hidden_ref[...]
    mixf = (spread * downf).astype(bf16)
    result_ref[...] = (hidden + (total + nn(mixf, bf_scr[...]))).astype(bf16)
    gdowni = (spread * sidei).astype(bf16)
    logit = logit_gradient(downf * sidef_ref[...] + downi_ref[...] * sidei, spread, group_ref[...], pick_ref[...])
    pair = jnp.concatenate([gdowni, logit], 1)
    grad_normed = back + nn(pair, down_scr[...])
    scale = lax.rsqrt(jnp.mean(hidden * hidden, -1, keepdims=True) + EPS)
    weighted = grad_normed * gain_ref[...].astype(f32)
    inner = jnp.mean(weighted * hidden, -1, keepdims=True)
    ghidden = cot.astype(f32) + scale * weighted - hidden * (scale * scale * scale * inner)
    ghidden_ref[...] = ghidden
    branch = ghidden.astype(bf16)
    attended = jnp.concatenate([aa_ref[...], ab_ref[...]], 1)
    sideo = nt(branch, bo_scr[...])
    gdowno = (spread1_ref[...] * sideo).astype(bf16)
    prod_ref[...] = downo_ref[...] * sideo
    gatt = (nt(branch, wo_scr[...]) + nn(gdowno, ao_scr[...])).astype(bf16)
    ga_ref[...] = gatt[:, :384]
    gb_ref[...] = gatt[:, 384:]
    pair_acc[...] += tn(pair, normed)
    bff_acc[...] += tn(mixf, cot)
    bo_acc[...] += tn(mixo_ref[...], branch)
    ao_acc[...] += tn(gdowno, attended)
    gain_acc[...] += jnp.sum(grad_normed * hidden * scale, 0, keepdims=True)

    @pl.when(step == pl.num_programs(0) - 1)
    def _():
        ao_grad[...] = ao_acc[:LORA]
        quarters = (pair_acc[:LORA], bff_acc[:LORA], bo_acc[:LORA], router_quarter(pair_acc, gain_acc))
        for j in range(4):
            source, at = (shard_ref, j) if j < 2 else (shard_acc, j - 2)
            pieces[j, 0:LORA] = source[at, 0]
            pieces[j, LORA : 2 * LORA] = source[at, 1]
            pieces[jnp.bitwise_xor(place[0], j), 2 * LORA : 3 * LORA] = quarters[j]
        send_pieces(pieces, own_ref, (sent1, sent2, sent3))


def router_quarter(pair_acc, gain_acc):
    gain = jnp.broadcast_to(gain_acc[...], (8, MODEL_WIDTH))
    return jnp.concatenate([pair_acc[LANES : LANES + 16, :], gain, jnp.zeros((16, MODEL_WIDTH), f32)], 0)


def last_kernel(
    place, x_ref, gain_ref, normed_ref, mixed_ref, spread_ref, downs_ref, prod_ref, ghidden_ref, downs_in, router_ref,
    dqa, dka, dva, dqb, dkb, dvb, joined_a, ups_a, joined_b, ups_b, group_ref, pick_ref, ta_ref, tb_ref, ao_grad,
    before_ref,
    gtokens_ref, own_ref, sent1, sent2, sent3, down_scr, pair_acc, up_acc, gain_acc, pieces,
):
    step = pl.program_id(0)

    @pl.when(step == 0)
    def _():
        down_scr[...] = down_rows([downs_in[0], downs_in[1], downs_in[2]], router_ref[...])
        pair_acc[...] = jnp.zeros_like(pair_acc)
        up_acc[...] = jnp.zeros_like(up_acc)
        gain_acc[...] = jnp.zeros_like(gain_acc)

    side_a = jnp.concatenate([dqa[...], dka[...], dva[...]], 1)
    side_b = jnp.concatenate([dqb[...], dkb[...], dvb[...]], 1)
    normed = normed_ref[...]
    mixed = mixed_ref[...]
    side = nt(side_a, ups_a[...]) + nt(side_b, ups_b[...])
    spread = spread_ref[...]
    gdown = (spread * side).astype(bf16)
    gates = jnp.where(lane_index(spread.shape) < LORA, spread, 0.0)
    logit = logit_gradient(downs_ref[...] * side + prod_ref[...], gates, group_ref[...], pick_ref[...])
    pair = jnp.concatenate([gdown, logit], 1)
    grad_normed = nn(side_a, joined_a[...]) + nn(side_b, joined_b[...]) + nn(pair, down_scr[...])
    x = x_ref[...].astype(f32)
    scale = lax.rsqrt(jnp.mean(x * x, -1, keepdims=True) + EPS)
    weighted = grad_normed * gain_ref[...].astype(f32)
    inner = jnp.mean(weighted * x, -1, keepdims=True)
    gtokens_ref[...] = (ghidden_ref[...] + scale * weighted - x * (scale * scale * scale * inner)).astype(bf16)
    pair_acc[...] += tn(pair, normed)
    up_acc[0] += tn(mixed, side_a)
    up_acc[1] += tn(mixed, side_b)
    gain_acc[...] += jnp.sum(grad_normed * x * scale, 0, keepdims=True)

    @pl.when(step == pl.num_programs(0) - 1)
    def _():
        quarters = (
            pair_acc[0:LORA],
            pair_acc[LORA : 2 * LORA],
            pair_acc[2 * LORA : 3 * LORA],
            router_quarter(pair_acc, gain_acc),
        )
        for j in range(4):
            half, odd = j // 2, j % 2
            parts = [ao_grad[:, 192 * j : 192 * j + 192]]
            for part in range(3):
                first = 384 * part + 192 * odd
                parts.append(up_acc[half, LORA * part : LORA * part + LORA, first : first + 192])
            pieces[j, 0:LORA] = jnp.concatenate(parts, 1)
            pieces[jnp.bitwise_xor(place[0], j), LORA : 2 * LORA] = quarters[j]
            table_ref = ta_ref if half == 0 else tb_ref
            rows = [table_ref[(3 * odd + i) // 2, (3 * odd + i) % 2 : (3 * odd + i) % 2 + 1, :] for i in range(3)]
            rows = jnp.concatenate(rows + [jnp.zeros((5, LANES), f32)], 0)
            pieces[j, 2 * LORA : 2 * LORA + 8] = jnp.concatenate([rows, jnp.zeros((8, MODEL_WIDTH - LANES), f32)], 1)
        send_pieces(pieces, own_ref, (sent1, sent2, sent3))


FF_ROWS, AT_ROWS, FLAT_ROWS = 120, 88, 1280
CHUNK = FLAT_ROWS // 8


def spread_kernel(place, own, one, two, three, out_ref):
    j = pl.program_id(0)
    for k, source in enumerate((own, one, two, three)):

        @pl.when(j == k)
        def _():
            out_ref[...] = source[...]


def scatter_kernel(spot, ff0, ff1, ff2, ff3, at0, at1, at2, at3, *refs):
    outs, flat = refs[:8], refs[8]
    ff = ff0[...] + ff1[...].astype(f32) + ff2[...].astype(f32) + ff3[...].astype(f32)
    at = at0[...] + at1[...].astype(f32) + at2[...].astype(f32) + at3[...].astype(f32)
    rows = FF_ROWS + AT_ROWS
    for t in range(6):
        flat[rows * t : rows * t + FF_ROWS, :] = ff[:, LANES * t : LANES * t + LANES]
        flat[rows * t + FF_ROWS : rows * t + rows, :] = at[:, LANES * t : LANES * t + LANES]
    flat[6 * rows :, :] = jnp.zeros((FLAT_ROWS - 6 * rows, LANES), f32)
    for k, out in enumerate(outs):
        first = pl.multiple_of(CHUNK * jnp.bitwise_xor(spot[0], k), CHUNK)
        out[...] = flat[pl.ds(first, CHUNK), :].astype(out.dtype)


def gather_kernel(spot, *refs):
    pieces, out = refs[:8], refs[8]
    for k, piece in enumerate(pieces):
        first = pl.multiple_of(CHUNK * jnp.bitwise_xor(spot[0], k), CHUNK)
        out[pl.ds(first, CHUNK), :] = piece[...]


def unpack_kernel(
    place, own, one, two, three, gain1_ref, gain2_ref, qkv_ref, bq_ref, bkv_ref, ao_ref, bo_ref, ai_ref, bi_ref,
    aff_ref, bff_ref, r1_ref, r2_ref, table_ref, quarters2, quarters1,
):
    rows = FF_ROWS + AT_ROWS

    def piece(ref, first, count):
        return jnp.concatenate([ref[rows * t + first : rows * t + first + count, :] for t in range(6)], 1).astype(f32)

    m = place[0]
    bi_ref[...] = piece(own, 0, LORA)
    mine = piece(own, FF_ROWS, LORA)
    bq_ref[...] = mine[:, 192:384]
    bkv_ref[0] = mine[:, 384:576]
    bkv_ref[1] = mine[:, 576:768]
    table_ref[...] = own[FF_ROWS + 2 * LORA : FF_ROWS + 2 * LORA + 8, :].astype(f32)[:3, :BUCKETS]
    for j, ref in enumerate((own, one, two, three)):
        there = jnp.bitwise_xor(m, j)
        quarters2[there] = piece(ref, 2 * LORA, LORA)
        quarters1[there] = piece(ref, FF_ROWS + LORA, LORA)
        low = piece(ref, LORA, LORA)
        out = piece(ref, FF_ROWS, LORA)[:, :192]
        for at in range(4):

            @pl.when(there == at)
            def _():
                aff_ref[:, MODEL_WIDTH * at : MODEL_WIDTH * at + MODEL_WIDTH] = low
                ao_ref[:, 192 * at : 192 * at + 192] = out

    for part in range(3):
        qkv_ref[part] = quarters1[part]
    ai_ref[...] = quarters2[0]
    bff_ref[...] = quarters2[1]
    bo_ref[...] = quarters2[2]
    r1_ref[...] = quarters1[3, :EXPERTS]
    r2_ref[...] = quarters2[3, :EXPERTS]
    gain1_ref[...] = quarters1[3, 16:17]
    gain2_ref[...] = quarters2[3, 16:17]


def whole(array):
    return pl.BlockSpec(array.shape, lambda *_: (0,) * array.ndim)


def rows_block(array):
    return pl.BlockSpec((HALF_ROWS, array.shape[1]), lambda i, *_: (i, 0))


def token_block():
    return pl.BlockSpec((HALF_ROWS, MODEL_WIDTH), lambda i, place, *_: (place[0] + 4 * i, 0))


def pair_block():
    return pl.BlockSpec((ROWS, LANES), lambda p, *_: (0, p))


def shape(dims, dtype):
    return jax.ShapeDtypeStruct(dims, dtype)


def call(kernel, grid, scalars, inputs, in_specs, outs, out_specs, scratch=(), flops=0, moved=0):
    return pl.pallas_call(
        kernel,
        grid_spec=pltpu.PrefetchScalarGridSpec(
            num_scalar_prefetch=len(scalars),
            grid=grid,
            in_specs=in_specs,
            out_specs=out_specs,
            scratch_shapes=list(scratch),
        ),
        out_shape=outs,
        compiler_params=pltpu.CompilerParams(vmem_limit_bytes=VMEM_LIMIT),
        cost_estimate=pl.CostEstimate(flops=flops, bytes_accessed=moved, transcendentals=0),
    )(*scalars, *inputs)


def exchange(value, axis, size, mask):
    return lax.ppermute(value, axis, [(i, i ^ mask) for i in range(size)])


def sum_over(value, axis, size, index, first_bit):
    def digits(v, low):
        if (1 << low) >= size:
            return v
        bits = min(3, size.bit_length() - 1 - low)
        count = 1 << bits
        digit = (index >> low) & (count - 1)
        parts = v.reshape(count, -1, v.shape[-1])
        mine = lax.dynamic_index_in_dim(parts, digit, 0, False)
        for k in range(1, count):
            piece = lax.dynamic_index_in_dim(parts, digit ^ k, 0, False)
            mine = mine + exchange(piece, axis, size, k << low)
        mine = digits(mine, low + bits)
        pieces = [mine] + [exchange(mine, axis, size, k << low) for k in range(1, count)]
        stacked = jnp.stack(pieces)
        order = digit ^ jnp.arange(count)
        return jnp.take(stacked, order, axis=0).reshape(v.shape)

    return digits(value, first_bit)


def constants():
    group1 = np.zeros((LANES, LANES), np.float32)
    for i in range(3 * LORA):
        for j in range(LORA):
            group1[i, j] = float((i % LORA) // ADAPTER_RANK == j // ADAPTER_RANK)
    pick = np.zeros((LANES, LANES), np.float32)
    for e in range(EXPERTS):
        pick[ADAPTER_RANK * e, e] = 1.0
    turn = np.eye(LANES, dtype=np.float32)[::-1].copy()
    return tuple(jnp.asarray(c, bf16) for c in (group1, pick, turn))


def local(
    dp_size,
    mp_size,
    tokens,
    cotangent,
    attention_norm_gain,
    feedforward_norm_gain,
    query_projection_weight,
    key_value_weight,
    attention_output_weight,
    ffn_input_weight,
    ffn_output_weight,
    projection_down_weight,
    query_up_weight,
    key_value_up_weight,
    attention_output_down_weight,
    attention_output_up_weight,
    ffn_input_down_weight,
    ffn_input_up_weight,
    ffn_output_down_weight,
    ffn_output_up_weight,
    attention_router_weight,
    feedforward_router_weight,
    bucket_bias_table,
    offset_bucket_map,
    sequence_length_list,
):
    m = lax.axis_index("mp").astype(jnp.int32)
    d = lax.axis_index("dp").astype(jnp.int32)
    place = m.reshape(1)
    spot = (d & 7).reshape(1)
    group, pick, turn = constants()

    def mp_swap(value, mask):
        return exchange(value, "mp", mp_size, mask)

    def pack_part(rows, index):
        return pl.BlockSpec((rows, MODEL_WIDTH), lambda *_: (index, 0))

    inputs = [
        query_projection_weight.T,
        jnp.transpose(key_value_weight, (0, 2, 1)),
        attention_output_weight,
        query_up_weight,
        key_value_up_weight,
        bucket_bias_table.T,
        ffn_input_up_weight,
    ]
    pack_shape = shape((PACK_ROWS, MODEL_WIDTH), bf16)
    pack0 = call(
        pack_kernel, (1,), [], inputs, [whole(a) for a in inputs], pack_shape, whole(pack_shape), moved=3_000_000
    )
    pack2 = mp_swap(pack0, 2)
    pack1 = mp_swap(pack0, 1)
    win0, wout0 = ffn_input_weight, ffn_output_weight
    win2, wout2 = mp_swap(win0, 2), mp_swap(wout0, 2)
    pack3 = mp_swap(pack2, 1)
    win1, wout1 = mp_swap(win0, 1), mp_swap(wout0, 1)
    win3, wout3 = mp_swap(win2, 1), mp_swap(wout2, 1)

    gain1 = attention_norm_gain.reshape(1, -1)
    gain2 = feedforward_norm_gain.reshape(1, -1)
    downs_in = jnp.transpose(projection_down_weight, (0, 2, 1))
    router1, router2 = attention_router_weight.T, feedforward_router_weight.T
    rev_map = jnp.concatenate([offset_bucket_map[::-1], jnp.full((1,), -1, jnp.int32)]).reshape(1, -1)

    wide, narrow = shape((ROWS, MODEL_WIDTH), bf16), shape((ROWS, LANES), f32)
    narrow16, half16 = shape((ROWS, LANES), bf16), shape((ROWS, 384), bf16)
    joined_shape, ups_shape = shape((1152, MODEL_WIDTH), bf16), shape((LANES, 1152), bf16)

    outs = [wide, narrow16, narrow, narrow, half16, half16, half16, joined_shape, ups_shape]
    normed1, mixed1, spread1, downs1, qa, ka, va, joined_a, ups_a = call(
        first_kernel,
        (2,),
        [place],
        [tokens, gain1, downs_in, router1, pack0, pack0, pack1, pack1],
        [token_block(), whole(gain1), whole(downs_in), whole(router1)] + [pack_part(576, 0), pack_part(48, 16)] * 2,
        outs,
        [rows_block(o) for o in outs[:-2]] + [whole(o) for o in outs[-2:]],
        scratch=[pltpu.VMEM((256, MODEL_WIDTH), bf16)],
        flops=2 * ROWS * 768 * 1536,
        moved=10_000_000,
    )

    def attend(q, k, v, one, two):
        return call(
            forward_attention,
            (3,),
            [place, sequence_length_list],
            [q, k, v, one, two, rev_map],
            [pair_block(), pair_block(), pair_block(), pack_part(48, 16), pack_part(48, 16), whole(rev_map)],
            [half16, shape((3, 8, 256), f32), shape((3, 7, LANES, 256), bf16)],
            [
                pair_block(),
                pl.BlockSpec((1, 8, 256), lambda p, *_: (p, 0, 0)),
                pl.BlockSpec((1, 7, LANES, 256), lambda p, *_: (p, 0, 0, 0)),
            ],
            flops=2 * 2 * 6 * 64 * (512 * 512 + 4 * 128 * 128) * 3,
            moved=6_000_000,
        )

    attended_a, lse_a, tiles_a = attend(qa, ka, va, pack0, pack1)
    outs = [half16, half16, half16, joined_shape, ups_shape]
    qb, kb, vb, joined_b, ups_b = call(
        second_kernel,
        (2,),
        [],
        [normed1, mixed1, pack2, pack2, pack3, pack3],
        [rows_block(normed1), rows_block(mixed1)] + [pack_part(576, 0), pack_part(48, 16)] * 2,
        outs,
        [rows_block(o) for o in outs[:-2]] + [whole(o) for o in outs[-2:]],
        flops=2 * ROWS * 768 * 1280,
        moved=8_000_000,
    )
    attended_b, lse_b, tiles_b = attend(qb, kb, vb, pack2, pack3)

    packs = [pack0, pack1, pack2, pack3]
    ao_in, bo_in, bf_in = attention_output_down_weight.T, attention_output_up_weight, ffn_output_up_weight
    down_in, low_in = ffn_input_down_weight.T, ffn_output_down_weight.T

    def low_block(j):
        return pl.BlockSpec((LORA, MODEL_WIDTH), lambda i, place, *_: (0, jnp.bitwise_xor(place[0], j)))

    def shard_inputs(first, wins, wouts):
        values, specs = [], []
        for j in range(2):
            values += [wins[j], packs[first + j], wouts[j], low_in]
            specs += [whole(wins[j]), pack_part(48, 17), whole(wouts[j]), low_block(first + j)]
        return values, specs

    shards_shape = shape((2, 2, LORA, MODEL_WIDTH), f32)
    wide_f32 = shape((ROWS, MODEL_WIDTH), f32)
    states = [wide_f32, wide, narrow, narrow16, narrow16, narrow, narrow, narrow, narrow16]
    states += [wide_f32, narrow, wide_f32, narrow]
    map_scratch = [
        pltpu.VMEM((LANES, MODEL_WIDTH), bf16),
        pltpu.VMEM((LANES, MODEL_WIDTH), bf16),
        pltpu.VMEM((MODEL_WIDTH, MODEL_WIDTH), bf16),
        pltpu.VMEM((256, MODEL_WIDTH), bf16),
        pltpu.VMEM((LANES, MODEL_WIDTH), bf16),
        pltpu.VMEM((2, LANES, MODEL_WIDTH), bf16),
        pltpu.VMEM((2, LANES, MODEL_WIDTH), bf16),
    ]
    maps = packs + [ao_in, bo_in, spread1, gain2, down_in, router2, bf_in]
    map_specs = [pack_part(192, 3)] * 4 + [whole(ao_in), whole(bo_in), rows_block(spread1), whole(gain2)]
    map_specs += [whole(down_in), whole(router2), whole(bf_in)]
    values, specs = shard_inputs(0, (win0, win1), (wout0, wout1))
    state = call(
        middle_kernel,
        (2,),
        [place],
        [tokens, cotangent, attended_a, attended_b] + maps + values,
        [token_block(), token_block(), rows_block(attended_a), rows_block(attended_b)] + map_specs + specs,
        states + [shards_shape],
        [rows_block(s) for s in states] + [whole(shards_shape)],
        scratch=map_scratch,
        flops=12_000_000_000,
        moved=30_000_000,
    )
    state, shard_grads = state[:-1], state[-1]

    values, specs = shard_inputs(2, (win2, win3), (wout2, wout3))
    ao_shape = shape((LORA, MODEL_WIDTH), f32)
    ff_shapes = [shape((FF_ROWS, MODEL_WIDTH), f32)] + [shape((FF_ROWS, MODEL_WIDTH), bf16)] * 3
    outs = [wide, wide_f32, half16, half16, narrow, ao_shape] + ff_shapes
    result, ghidden, ga, gb, prod, ao_grad, *ff_pieces = call(
        post_kernel,
        (2,),
        [place],
        [cotangent, attended_a, attended_b] + maps + values + [group, pick] + list(state) + [shard_grads],
        [token_block(), rows_block(attended_a), rows_block(attended_b)]
        + map_specs
        + specs
        + [whole(group), whole(pick)]
        + [rows_block(s) for s in state]
        + [whole(shard_grads)],
        outs,
        [rows_block(o) for o in outs[:5]] + [whole(o) for o in outs[5:]],
        scratch=map_scratch
        + [
            pltpu.VMEM((2, 2, LORA, MODEL_WIDTH), f32),
            pltpu.VMEM((256, MODEL_WIDTH), f32),
            pltpu.VMEM((LANES, MODEL_WIDTH), f32),
            pltpu.VMEM((LANES, MODEL_WIDTH), f32),
            pltpu.VMEM((LANES, MODEL_WIDTH), f32),
            pltpu.VMEM((1, MODEL_WIDTH), f32),
            pltpu.VMEM((4, FF_ROWS, MODEL_WIDTH), f32),
        ],
        flops=14_000_000_000,
        moved=40_000_000,
    )
    result2 = mp_swap(result, 2)
    ff_parts = [ff_pieces[0]] + [mp_swap(ff_pieces[j], j) for j in (1, 2, 3)]

    def attend_back(q, k, v, do, lse, tiles):
        return call(
            backward_attention,
            (3,),
            [place, sequence_length_list],
            [q, k, v, do, lse, tiles, rev_map, turn],
            [pair_block()] * 4
            + [
                pl.BlockSpec((1, 8, 256), lambda p, *_: (p, 0, 0)),
                pl.BlockSpec((1, 7, LANES, 256), lambda p, *_: (p, 0, 0, 0)),
                whole(rev_map),
                whole(turn),
            ],
            [half16, half16, half16, shape((3, 8, LANES), f32)],
            [pair_block()] * 3 + [pl.BlockSpec((1, 8, LANES), lambda p, *_: (p, 0, 0))],
            scratch=[
                pltpu.VMEM((LONG_LEN, 1024), bf16),
                pltpu.VMEM((LONG_LEN, 1024), bf16),
                pltpu.VMEM((1024, LANES), bf16),
                pltpu.VMEM((1024, LANES), bf16),
                pltpu.VMEM((7, LANES, 256), f32),
            ],
            flops=2 * 5 * 6 * 64 * (512 * 512 + 4 * 128 * 128) * 3,
            moved=8_000_000,
        )

    dqa, dka, dva, table_a = attend_back(qa, ka, va, ga, lse_a, tiles_a)
    dqb, dkb, dvb, table_b = attend_back(qb, kb, vb, gb, lse_b, tiles_b)

    rows_in = [normed1, mixed1, spread1, downs1, prod, ghidden]
    grads_in = [dqa, dka, dva, dqb, dkb, dvb]
    fixed = [joined_a, ups_a, joined_b, ups_b, group, pick, table_a, table_b, ao_grad]
    at_shapes = [shape((AT_ROWS, MODEL_WIDTH), f32)] + [shape((AT_ROWS, MODEL_WIDTH), bf16)] * 3
    gtokens, *at_pieces = call(
        last_kernel,
        (2,),
        [place],
        [tokens, gain1] + rows_in + [downs_in, router1] + grads_in + fixed + [result2],
        [token_block(), whole(gain1)]
        + [rows_block(a) for a in rows_in]
        + [whole(downs_in), whole(router1)]
        + [rows_block(a) for a in grads_in]
        + [whole(a) for a in fixed]
        + [pl.BlockSpec(memory_space=pl.ANY)],
        [wide] + at_shapes,
        [rows_block(wide)] + [whole(o) for o in at_shapes],
        scratch=[
            pltpu.VMEM((256, MODEL_WIDTH), bf16),
            pltpu.VMEM((256, MODEL_WIDTH), f32),
            pltpu.VMEM((2, LANES, 1152), f32),
            pltpu.VMEM((1, MODEL_WIDTH), f32),
            pltpu.VMEM((4, AT_ROWS, MODEL_WIDTH), f32),
        ],
        flops=6_000_000_000,
        moved=20_000_000,
    )
    gtokens2 = mp_swap(gtokens, 2)
    at_parts = [at_pieces[0]] + [mp_swap(at_pieces[j], j) for j in (1, 2, 3)]

    def spread_rows(own, two):
        one = mp_swap(own, 1)
        three = mp_swap(two, 1)

        def source(k):
            return pl.BlockSpec(
                (HALF_ROWS, MODEL_WIDTH), lambda j, part, *_: (jnp.where(j == k, part, jnp.where(j < k, 0, 1)), 0)
            )

        return call(
            spread_kernel,
            (4, 2),
            [place],
            [own, one, two, three],
            [source(k) for k in range(4)],
            shape((4 * ROWS, MODEL_WIDTH), bf16),
            pl.BlockSpec(
                (HALF_ROWS, MODEL_WIDTH), lambda j, part, place, *_: (4 * part + jnp.bitwise_xor(place[0], j), 0)
            ),
            moved=12_000_000,
        )

    output = spread_rows(result, result2)
    grad_tokens = spread_rows(gtokens, gtokens2)

    chunk, chunk16 = shape((CHUNK, LANES), f32), shape((CHUNK, LANES), bf16)
    flat_shape = shape((FLAT_ROWS, LANES), bf16)
    parts = ff_parts + at_parts
    mine, *others = call(
        scatter_kernel,
        (1,),
        [spot],
        parts,
        [whole(a) for a in parts],
        [chunk] + [chunk16] * 7,
        [whole(chunk)] * 8,
        scratch=[pltpu.VMEM((FLAT_ROWS, LANES), f32)],
        moved=3_000_000,
    )
    for k in range(1, 8):
        mine = mine + exchange(others[k - 1], "dp", dp_size, k).astype(f32)
    mine = sum_over(mine, "dp", dp_size, d, 3).astype(bf16)
    pieces = [mine] + [exchange(mine, "dp", dp_size, k) for k in range(1, 8)]
    own = call(
        gather_kernel, (1,), [spot], pieces, [whole(a) for a in pieces], flat_shape, whole(flat_shape), moved=700_000
    )
    two = mp_swap(own, 2)
    one = mp_swap(own, 1)
    three = mp_swap(two, 1)
    outs = [
        shape((1, MODEL_WIDTH), f32),
        shape((1, MODEL_WIDTH), f32),
        shape((3, LORA, MODEL_WIDTH), f32),
        shape((LORA, 192), f32),
        shape((2, LORA, 192), f32),
        shape((LORA, MODEL_WIDTH), f32),
        shape((LORA, MODEL_WIDTH), f32),
        shape((LORA, MODEL_WIDTH), f32),
        shape((LORA, MODEL_WIDTH), f32),
        shape((LORA, 4 * MODEL_WIDTH), f32),
        shape((LORA, MODEL_WIDTH), f32),
        shape((EXPERTS, MODEL_WIDTH), f32),
        shape((EXPERTS, MODEL_WIDTH), f32),
        shape((3, BUCKETS), f32),
    ]
    flats = [own, one, two, three]
    grads = call(
        unpack_kernel,
        (1,),
        [place],
        flats,
        [whole(a) for a in flats],
        outs,
        [whole(o) for o in outs],
        scratch=[pltpu.VMEM((4, LORA, MODEL_WIDTH), f32)] * 2,
        moved=3_000_000,
    )
    g1, g2, g_qkv, g_bq, g_bkv, g_ao, g_bo, g_ai, g_bi, g_aff, g_bff, g_r1, g_r2, g_table = grads
    return (
        output,
        grad_tokens,
        g1.reshape(-1),
        g2.reshape(-1),
        jnp.transpose(g_qkv, (0, 2, 1)),
        g_bq,
        g_bkv,
        g_ao.T,
        g_bo,
        g_ai.T,
        g_bi,
        g_aff.T,
        g_bff,
        g_r1.T,
        g_r2.T,
        g_table.T,
    )


def solution(mesh):
    in_specs = (
        P("dp", None),
        P("dp", None),
        P(),
        P(),
        P(None, "mp"),
        P(None, None, "mp"),
        P("mp", None),
        P(None, "mp"),
        P("mp", None),
        P(),
        P(None, "mp"),
        P(None, None, "mp"),
        P(),
        P(),
        P(),
        P(None, "mp"),
        P(),
        P(),
        P(),
        P(),
        P(None, "mp"),
        P(),
        P("dp"),
    )
    out_specs = (
        P("dp", None),
        P("dp", None),
        P(),
        P(),
        P(),
        P(None, "mp"),
        P(None, None, "mp"),
        P(),
        P(),
        P(),
        P(None, "mp"),
        P(),
        P(),
        P(),
        P(),
        P(None, "mp"),
    )
    step = functools.partial(local, mesh.shape["dp"], mesh.shape["mp"])
    return jax.shard_map(step, mesh=mesh, in_specs=in_specs, out_specs=out_specs, check_vma=False)
```

time: 2480 us -> 397 us (0.16)
  local copies, waits for them, and re-layouts: 1060 us -> 5.86 us
  waiting for transfers between devices: 1010 us -> 174 us
  matrix products: 294 us -> 0 us
  Pallas kernels: 0 us -> 171 us
  other arithmetic: 86.4 us -> 4.18 us
  starting transfers between devices: 0.25 us -> 33.4 us
    psum x6 -> x0, waiting for transfers between devices: 1010 us -> none  [the longest x1 439 us: local(): lax.psum((matrix_product(ffn_state['active'], ffout_all), matrix_product(...]
    gather x2 -> x0, local copies, waits for them, and re-layouts: 933 us -> none  [local(): pos_bias = jnp.transpose(jnp.take(rel_bias, offsets, axis=0), (2, 0, 1))]
    dot_general x111 -> x0, matrix products: 294 us -> none  [the longest x36 120 us: product_with_transpose(): lax.dot_general(left_op, right_op, (((1,), (1,)), ((), ())), preferred_el...]
    ppermute x0 -> x38, waiting for transfers between devices: none -> 174 us  [exchange(): return lax.ppermute(value, axis, [(i, i ^ mask) for i in range(size)])]
    pallas_call x0 -> x15, Pallas kernels: none -> 171 us  [call(): pl.pallas_call(kernel, grid_spec=pltpu.PrefetchScalarGridSpec(num_scalar_...]
    unnamed x459 -> x52, local copies, waits for them, and re-layouts: 54 us -> 4.69 us
    ppermute x0 -> x38, starting transfers between devices: none -> 33.4 us  [exchange(): return lax.ppermute(value, axis, [(i, i ^ mask) for i in range(size)])]
    reduce_sum x25 -> x0, other arithmetic: 32.5 us -> none  [the longest x2 11.5 us: attend_backward(): bias_part = jnp.sum(grad_scores.astype(single_precision), 0)]
  transfers between devices with their start and end apart: 6 -> 38, of which waited for: 6 -> 20; matrix products, arithmetic and copies ran while one was open for 4% -> 1% of each run, Pallas kernels for 0% -> 29%
where the time goes in v1:
time: 397 us; the launch traced here: 390 us
  waiting for transfers between devices  174 us (44%)
  Pallas kernels  171 us (43%)
  starting transfers between devices  33.4 us (8%)
  local copies, waits for them, and re-layouts  5.86 us (1%)
  other arithmetic  4.18 us (1%)
    ppermute x38, waiting for transfers between devices, exchange(): return lax.ppermute(value, axis, [(i, i ^ mask) for i in range(size)])  174 us
    pallas_call x15, Pallas kernels, call(): pl.pallas_call(kernel, grid_spec=pltpu.PrefetchScalarGridSpec(num_scalar_...  171 us
    ppermute x38, starting transfers between devices, exchange(): return lax.ppermute(value, axis, [(i, i ^ mask) for i in range(size)])  33.4 us
  transfers between devices with their start and end apart: 38, of which 20 were waited for; matrix products, arithmetic and copies ran while one was open for 1% of the time, Pallas kernels for 29%

profile of v1, /device:TPU:0, one launch (start us, length us, event | category | flops | bytes accessed | tf_op | source)
XLA Modules:
  0.0 389.9 jit_solution(11087807241283204966)
XLA Ops:
  8.1 28.1 %collective-permute-done.1.one_ref.ups_one.wo2.up0 = bf16[864,768]{1,0:T(8,128)(2,1)S(1)} collective-permute-done((bf16[864,768]{1,0:T(8,128)(2,1)}, bf16[864,768]{1,0:T(8,128)(2,1)S(1)}, u32[]{:S(2)}, u32[]{:S(2)}) %collective-permute-start.1) | collective-permute-done | bytes 1327136 | tf_op jit(solution)/shard_map/ppermute | solution.py:630
  36.7 24.9 %collective-permute-done.3.win0 = bf16[768,768]{1,0:T(8,128)(2,1)} collective-permute-done((bf16[768,768]{1,0:T(8,128)(2,1)}, bf16[768,768]{1,0:T(8,128)(2,1)}, u32[]{:S(2)}, u32[]{:S(2)}) %collective-permute-start.3) | collective-permute-done | bytes 1179680 | tf_op jit(solution)/shard_map/ppermute | solution.py:630
  63.6 22.5 %collective-permute-done.4.wout0 = bf16[768,768]{1,0:T(8,128)(2,1)} collective-permute-done((bf16[768,768]{1,0:T(8,128)(2,1)}, bf16[768,768]{1,0:T(8,128)(2,1)}, u32[]{:S(2)}, u32[]{:S(2)}) %collective-permute-start.4) | collective-permute-done | bytes 1179680 | tf_op jit(solution)/shard_map/ppermute | solution.py:630
  87.2 8.9 %shard_map.370 = (bf16[1024,768]{1,0:T(8,128)(2,1)}, bf16[1024,128]{1,0:T(8,128)(2,1)}, f32[1024,128]{1,0:T(8,128)}, f32[1024,128]{1,0:T(8,128)}, bf16[1024,384]...) custom-call(s32[1]{0:T(128)} %bitcast.place, ...), custom_call_target="tpu_custom_call" | custom-call | flops 2415919104 | bytes 10000000 | tf_op jit(solution)/shard_map/pallas_call | solution.py:614
  96.0 11.2 %shard_map.371 = (bf16[1024,384]{1,0:T(8,128)(2,1)}, f32[3,8,256]{2,1,0:T(8,128)}, bf16[3,7,128,256]{3,2,1,0:T(8,128)(2,1)}) custom-call(s32[1]{0:T(128)} %bitcast.place, s32[20]{0:T(128)} %lengths.7, bf16[1024,384]{1,0:T(8,128)(2,1)} %get-tuple-element.95.q_ref, bf16[1024,384]{1,0:T(8,128)(2,1)} %get-tuple-element.96.k_ref, ...), custom_call_target="tpu_custom_call" | custom-call | flops 1509949440 | bytes 6000000 | tf_op jit(solution)/shard_map/pallas_call | solution.py:614
  107.2 6.2 %shard_map.372 = (bf16[1024,384]{1,0:T(8,128)(2,1)}, bf16[1024,384]{1,0:T(8,128)(2,1)}, bf16[1024,384]{1,0:T(8,128)(2,1)}, bf16[1152,768]{1,0:T(8,128)(2,1)}, bf16[128,1152]{1,0:T(8,128)(2,1)}) custom-call(bf16[1024,768]{1,0:T(8,128)(2,1)} %get-tuple-element.99.normed_ref, bf16[1024,128]{1,0:T(8,128)(2,1)} %get-tuple-element.100.mixed_ref, ...), custom_call_target="tpu_custom_call" | custom-call | flops 2013265920 | bytes 8000000 | tf_op jit(solution)/shard_map/pallas_call | solution.py:614
  113.5 11.1 %shard_map.373 = (bf16[1024,384]{1,0:T(8,128)(2,1)}, f32[3,8,256]{2,1,0:T(8,128)}, bf16[3,7,128,256]{3,2,1,0:T(8,128)(2,1)}) custom-call(s32[1]{0:T(128)} %bitcast.place, s32[20]{0:T(128)} %lengths.7, bf16[1024,384]{1,0:T(8,128)(2,1)} %get-tuple-element.101.q_ref, bf16[1024,384]{1,0:T(8,128)(2,1)} %get-tuple-element.102.k_ref, ...), custom_call_target="tpu_custom_call" | custom-call | flops 1509949440 | bytes 6000000 | tf_op jit(solution)/shard_map/pallas_call | solution.py:614
  124.6 29.8 %shard_map.374 = (f32[1024,768]{1,0:T(8,128)}, bf16[1024,768]{1,0:T(8,128)(2,1)}, f32[1024,128]{1,0:T(8,128)}, bf16[1024,128]{1,0:T(8,128)(2,1)}, bf16[1024,128]...) custom-call(s32[1]{0:T(128)} %bitcast.place, ...), custom_call_target="tpu_custom_call" | custom-call | flops 12000000000 | bytes 30000000 | tf_op jit(solution)/shard_map/pallas_call | solution.py:614
  155.8 32.0 %shard_map.375 = (bf16[1024,768]{1,0:T(8,128)(2,1)}, f32[1024,768]{1,0:T(8,128)}, bf16[1024,384]{1,0:T(8,128)(2,1)}, bf16[1024,384]{1,0:T(8,128)(2,1)}, f32[1024...) custom-call(s32[1]{0:T(128)} %bitcast.place, ...), custom_call_target="tpu_custom_call" | custom-call | flops 14000000000 | bytes 40000000 | tf_op jit(solution)/shard_map/pallas_call | solution.py:614
  189.5 15.2 %shard_map.378 = (bf16[1024,384]{1,0:T(8,128)(2,1)}, bf16[1024,384]{1,0:T(8,128)(2,1)}, bf16[1024,384]{1,0:T(8,128)(2,1)}, f32[3,8,128]{2,1,0:T(8,128)}) custom-call(s32[1]{0:T(128)} %bitcast.place, s32[20]{0:T(128)} %lengths.7, bf16[1024,384]{1,0:T(8,128)(2,1)} %get-tuple-element.101.q_ref, bf16[1024,384]{1,0:T(8,128)(2,1)} %get-tuple-element.102.k_ref, ...), custom_call_target="tpu_custom_call" | custom-call | flops 3774873600 | bytes 8000000 | tf_op jit(solution)/shard_map/pallas_call | solution.py:614
  204.7 14.9 %shard_map.377 = (bf16[1024,384]{1,0:T(8,128)(2,1)}, bf16[1024,384]{1,0:T(8,128)(2,1)}, bf16[1024,384]{1,0:T(8,128)(2,1)}, f32[3,8,128]{2,1,0:T(8,128)}) custom-call(s32[1]{0:T(128)} %bitcast.place, s32[20]{0:T(128)} %lengths.7, bf16[1024,384]{1,0:T(8,128)(2,1)} %get-tuple-element.95.q_ref, bf16[1024,384]{1,0:T(8,128)(2,1)} %get-tuple-element.96.k_ref, ...), custom_call_target="tpu_custom_call" | custom-call | flops 3774873600 | bytes 8000000 | tf_op jit(solution)/shard_map/pallas_call | solution.py:614
  219.6 5.5 %collective-permute-done.10.two.before_ref = bf16[1024,768]{1,0:T(8,128)(2,1)S(1)} collective-permute-done((bf16[1024,768]{1,0:T(8,128)(2,1)}, bf16[1024,768]{1,0:T(8,128)(2,1)S(1)}, u32[]{:S(2)}, u32[]{:S(2)}) %collective-permute-start.10) | collective-permute-done | bytes 1572896 | tf_op jit(solution)/shard_map/ppermute | solution.py:630
  226.2 15.2 %shard_map.379 = (bf16[1024,768]{1,0:T(8,128)(2,1)}, f32[88,768]{1,0:T(8,128)}, bf16[88,768]{1,0:T(8,128)(2,1)}, bf16[88,768]{1,0:T(8,128)(2,1)}, bf16[88,768]{1,0:T(8,128)(2,1)}) custom-call(s32[1]{0:T(128)} %bitcast.place, bf16[4096,768]{1,0:T(8,128)(2,1)} %x_ref.5, bf16[1,768]{1,0:T(2,128)(2,1)} %reshape.54.gain_ref, ...), custom_call_target="tpu_custom_call" | custom-call | flops 6000000000 | bytes 20000000 | tf_op jit(solution)/shard_map/pallas_call | solution.py:614
  245.7 37.2 %collective-permute-done.16.ff2 = bf16[120,768]{1,0:T(8,128)(2,1)S(1)} collective-permute-done((bf16[120,768]{1,0:T(8,128)(2,1)S(1)}, bf16[120,768]{1,0:T(8,128)(2,1)S(1)}, u32[]{:S(2)}, u32[]{:S(2)}) %collective-permute-start.16) | collective-permute-done | bytes 184352 | tf_op jit(solution)/shard_map/ppermute | solution.py:630
  286.1 3.7 collective-permute-done.19.at2
  310.1 4.5 %collective-permute-done.27 = bf16[160,128]{1,0:T(8,128)(2,1)S(1)} collective-permute-done((bf16[160,128]{1,0:T(8,128)(2,1)}, bf16[160,128]{1,0:T(8,128)(2,1)S(1)}, u32[]{:S(2)}, u32[]{:S(2)}) %collective-permute-start.27) | collective-permute-done | bytes 40992 | tf_op jit(solution)/shard_map/ppermute | solution.py:630
  318.1 4.3 %collective-permute-done.34.refs_7_ = bf16[160,128]{1,0:T(8,128)(2,1)S(1)} collective-permute-done((bf16[160,128]{1,0:T(8,128)(2,1)S(1)}, bf16[160,128]{1,0:T(8,128)(2,1)S(1)}, u32[]{:S(2)}, u32[]{:S(2)}) %collective-permute-start.34) | collective-permute-done | bytes 40992 | tf_op jit(solution)/shard_map/ppermute | solution.py:630
  328.6 6.2 %collective-permute-done.32.refs_5_ = bf16[160,128]{1,0:T(8,128)(2,1)S(1)} collective-permute-done((bf16[160,128]{1,0:T(8,128)(2,1)S(1)}, bf16[160,128]{1,0:T(8,128)(2,1)S(1)}, u32[]{:S(2)}, u32[]{:S(2)}) %collective-permute-start.32) | collective-permute-done | bytes 40992 | tf_op jit(solution)/shard_map/ppermute | solution.py:630
  334.8 4.9 %collective-permute-done.31.refs_4_ = bf16[160,128]{1,0:T(8,128)(2,1)S(1)} collective-permute-done((bf16[160,128]{1,0:T(8,128)(2,1)S(1)}, bf16[160,128]{1,0:T(8,128)(2,1)S(1)}, u32[]{:S(2)}, u32[]{:S(2)}) %collective-permute-start.31) | collective-permute-done | bytes 40992 | tf_op jit(solution)/shard_map/ppermute | solution.py:630
  339.7 4.9 %collective-permute-done.30.refs_3_ = bf16[160,128]{1,0:T(8,128)(2,1)S(1)} collective-permute-done((bf16[160,128]{1,0:T(8,128)(2,1)S(1)}, bf16[160,128]{1,0:T(8,128)(2,1)S(1)}, u32[]{:S(2)}, u32[]{:S(2)}) %collective-permute-start.30) | collective-permute-done | bytes 40992 | tf_op jit(solution)/shard_map/ppermute | solution.py:630
  344.6 4.0 %collective-permute-done.29.refs_2_ = bf16[160,128]{1,0:T(8,128)(2,1)S(1)} collective-permute-done((bf16[160,128]{1,0:T(8,128)(2,1)S(1)}, bf16[160,128]{1,0:T(8,128)(2,1)S(1)}, u32[]{:S(2)}, u32[]{:S(2)}) %collective-permute-start.29) | collective-permute-done | bytes 40992 | tf_op jit(solution)/shard_map/ppermute | solution.py:630
  356.1 6.1 %collective-permute-done.36.two = bf16[1280,128]{1,0:T(8,128)(2,1)S(1)} collective-permute-done((bf16[1280,128]{1,0:T(8,128)(2,1)}, bf16[1280,128]{1,0:T(8,128)(2,1)S(1)}, u32[]{:S(2)}, u32[]{:S(2)}) %collective-permute-start.36) | collective-permute-done | bytes 327712 | tf_op jit(solution)/shard_map/ppermute | solution.py:630
  371.8 8.7 %shard_map.376 = bf16[4096,768]{1,0:T(8,128)(2,1)} custom-call(s32[1]{0:T(128)} %bitcast.place, bf16[1024,768]{1,0:T(8,128)(2,1)} %get-tuple-element.120.own, bf16[1024,768]{1,0:T(8,128)(2,1)} %collective-permute-done.9.one, bf16[1024,768]{1,0:T(8,128)(2,1)} %copy-done, bf16[1024,768]{1,0:T(8,128)(2,1)} %collective-permute-done.11.three), custom_call_target="tpu_custom_call" | custom-call | bytes 12000000 | tf_op jit(solution)/shard_map/pallas_call | solution.py:614
  380.6 8.8 %shard_map.380 = bf16[4096,768]{1,0:T(8,128)(2,1)} custom-call(s32[1]{0:T(128)} %bitcast.place, bf16[1024,768]{1,0:T(8,128)(2,1)} %get-tuple-element.143.own, bf16[1024,768]{1,0:T(8,128)(2,1)} %collective-permute-done.12.one, bf16[1024,768]{1,0:T(8,128)(2,1)} %collective-permute-done.13.two, bf16[1024,768]{1,0:T(8,128)(2,1)} %collective-permute-done.14.three), custom_call_target="tpu_custom_call" | custom-call | bytes 12000000 | tf_op jit(solution)/shard_map/pallas_call | solution.py:614
  (125 shorter events, 69.5 us)
Async XLA Ops:
  3.1 33.1 %collective-permute-start.1 = (bf16[864,768]{1,0:T(8,128)(2,1)}, bf16[864,768]{1,0:T(8,128)(2,1)S(1)}, u32[]{:S(2)}, u32[]{:S(2)}) collective-permute-start(bf16[864,768]{1,0:T(8,128)(2,1)} %shard_map.369.one_ref.ups_one.wo0.up0), channel_id=1, source_target_pairs={{0,2},{1,3},{2,0},{3,1},{4,6},{5,7},{6,4},{7,5},{8,10},{9,11},{10,... | collective-permute-start | bytes 3981320 | tf_op jit(solution)/shard_map/ppermute | solution.py:630
  6.1 55.5 %collective-permute-start.3 = (bf16[768,768]{1,0:T(8,128)(2,1)}, bf16[768,768]{1,0:T(8,128)(2,1)}, u32[]{:S(2)}, u32[]{:S(2)}) collective-permute-start(bf16[768,768]{1,0:T(8,128)(2,1)} %win0.1), channel_id=1, source_target_pairs={{0,2},{1,3},{2,0},{3,1},{4,6},{5,7},{6,4},{7,5},{8,10},{9,11},{10,... | collective-permute-start | bytes 3538952 | tf_op jit(solution)/shard_map/ppermute | solution.py:630
  6.1 80.0 %collective-permute-start = (bf16[864,768]{1,0:T(8,128)(2,1)}, bf16[864,768]{1,0:T(8,128)(2,1)S(1)}, u32[]{:S(2)}, u32[]{:S(2)}) collective-permute-start(bf16[864,768]{1,0:T(8,128)(2,1)} %shard_map.369.one_ref.ups_one.wo0.up0), channel_id=1, source_target_pairs={{0,1},{1,0},{2,3},{3,2},{4,5},{5,4},{6,7},{7,6},{8,9},{9,8},{10,11... | collective-permute-start | bytes 3981320 | tf_op jit(solution)/shard_map/ppermute | solution.py:630
  6.1 80.0 %collective-permute-start.4 = (bf16[768,768]{1,0:T(8,128)(2,1)}, bf16[768,768]{1,0:T(8,128)(2,1)}, u32[]{:S(2)}, u32[]{:S(2)}) collective-permute-start(bf16[768,768]{1,0:T(8,128)(2,1)} %wout0.1), channel_id=1, source_target_pairs={{0,2},{1,3},{2,0},{3,1},{4,6},{5,7},{6,4},{7,5},{8,10},{9,11},{10,... | collective-permute-start | bytes 3538952 | tf_op jit(solution)/shard_map/ppermute | solution.py:630
  36.2 71.0 %collective-permute-start.2 = (bf16[864,768]{1,0:T(8,128)(2,1)S(1)}, bf16[864,768]{1,0:T(8,128)(2,1)}, u32[]{:S(2)}, u32[]{:S(2)}) collective-permute-start(bf16[864,768]{1,0:T(8,128)(2,1)S(1)} %collective-permute-done.1.one_ref.ups_one.wo2.up0), channel_id=1, source_target_pairs={{0,1},{1,0},{2,3},{3,2},{4,5},{5,4},{6,7},{7,6},{8,9},{9,8},{10,11... | collective-permute-start | bytes 3981320 | tf_op jit(solution)/shard_map/ppermute | solution.py:630
  36.2 88.4 %collective-permute-start.7 = (bf16[768,768]{1,0:T(8,128)(2,1)}, bf16[768,768]{1,0:T(8,128)(2,1)}, u32[]{:S(2)}, u32[]{:S(2)}) collective-permute-start(bf16[768,768]{1,0:T(8,128)(2,1)} %win0.1), channel_id=1, source_target_pairs={{0,1},{1,0},{2,3},{3,2},{4,5},{5,4},{6,7},{7,6},{8,9},{9,8},{10,11... | collective-permute-start | bytes 3538952 | tf_op jit(solution)/shard_map/ppermute | solution.py:630
  61.6 63.0 %collective-permute-start.8 = (bf16[768,768]{1,0:T(8,128)(2,1)}, bf16[768,768]{1,0:T(8,128)(2,1)}, u32[]{:S(2)}, u32[]{:S(2)}) collective-permute-start(bf16[768,768]{1,0:T(8,128)(2,1)} %wout0.1), channel_id=1, source_target_pairs={{0,1},{1,0},{2,3},{3,2},{4,5},{5,4},{6,7},{7,6},{8,9},{9,8},{10,11... | collective-permute-start | bytes 3538952 | tf_op jit(solution)/shard_map/ppermute | solution.py:630
  86.1 68.4 %collective-permute-start.5 = (bf16[768,768]{1,0:T(8,128)(2,1)}, bf16[768,768]{1,0:T(8,128)(2,1)S(1)}, u32[]{:S(2)}, u32[]{:S(2)}) collective-permute-start(bf16[768,768]{1,0:T(8,128)(2,1)} %collective-permute-done.3.win0), channel_id=1, source_target_pairs={{0,1},{1,0},{2,3},{3,2},{4,5},{5,4},{6,7},{7,6},{8,9},{9,8},{10,11... | collective-permute-start | bytes 3538952 | tf_op jit(solution)/shard_map/ppermute | solution.py:630
  86.1 68.4 %collective-permute-start.6 = (bf16[768,768]{1,0:T(8,128)(2,1)}, bf16[768,768]{1,0:T(8,128)(2,1)S(1)}, u32[]{:S(2)}, u32[]{:S(2)}) collective-permute-start(bf16[768,768]{1,0:T(8,128)(2,1)} %collective-permute-done.4.wout0), channel_id=1, source_target_pairs={{0,1},{1,0},{2,3},{3,2},{4,5},{5,4},{6,7},{7,6},{8,9},{9,8},{10,11... | collective-permute-start | bytes 3538952 | tf_op jit(solution)/shard_map/ppermute | solution.py:630
  187.9 37.2 %collective-permute-start.10 = (bf16[1024,768]{1,0:T(8,128)(2,1)}, bf16[1024,768]{1,0:T(8,128)(2,1)S(1)}, u32[]{:S(2)}, u32[]{:S(2)}) collective-permute-start(bf16[1024,768]{1,0:T(8,128)(2,1)} %get-tuple-element.120.own), channel_id=1, source_target_pairs={{0,2},{1,3},{2,0},{3,1},{4,6},{5,7},{6,4},{7,5},{8,10},{9,11},{10,... | collective-permute-start | bytes 4718600 | tf_op jit(solution)/shard_map/ppermute | solution.py:630
  241.4 65.9 %collective-permute-start.13 = (bf16[1024,768]{1,0:T(8,128)(2,1)}, bf16[1024,768]{1,0:T(8,128)(2,1)}, u32[]{:S(2)}, u32[]{:S(2)}) collective-permute-start(bf16[1024,768]{1,0:T(8,128)(2,1)} %get-tuple-element.143.own), channel_id=1, source_target_pairs={{0,2},{1,3},{2,0},{3,1},{4,6},{5,7},{6,4},{7,5},{8,10},{9,11},{10,... | collective-permute-start | bytes 4718600 | tf_op jit(solution)/shard_map/ppermute | solution.py:630
  243.1 39.8 %collective-permute-start.16 = (bf16[120,768]{1,0:T(8,128)(2,1)S(1)}, bf16[120,768]{1,0:T(8,128)(2,1)S(1)}, u32[]{:S(2)}, u32[]{:S(2)}) collective-permute-start(bf16[120,768]{1,0:T(8,128)(2,1)S(1)} %copy-done.23), channel_id=1, source_target_pairs={{0,2},{1,3},{2,0},{3,1},{4,6},{5,7},{6,4},{7,5},{8,10},{9,11},{10,... | collective-permute-start | bytes 552968 | tf_op jit(solution)/shard_map/ppermute | solution.py:630
  243.6 42.5 %collective-permute-start.17 = (bf16[120,768]{1,0:T(8,128)(2,1)}, bf16[120,768]{1,0:T(8,128)(2,1)}, u32[]{:S(2)}, u32[]{:S(2)}) collective-permute-start(bf16[120,768]{1,0:T(8,128)(2,1)} %get-tuple-element.147), channel_id=1, source_target_pairs={{0,3},{1,2},{2,1},{3,0},{4,7},{5,6},{6,5},{7,4},{8,11},{9,10},{10,... | collective-permute-start | bytes 552968 | tf_op jit(solution)/shard_map/ppermute | solution.py:630
  245.0 41.2 %collective-permute-start.18 = (bf16[88,768]{1,0:T(8,128)(2,1)}, bf16[88,768]{1,0:T(8,128)(2,1)}, u32[]{:S(2)}, u32[]{:S(2)}) collective-permute-start(bf16[88,768]{1,0:T(8,128)(2,1)} %get-tuple-element.149), channel_id=1, source_target_pairs={{0,1},{1,0},{2,3},{3,2},{4,5},{5,4},{6,7},{7,6},{8,9},{9,8},{10,11... | collective-permute-start | bytes 405512 | tf_op jit(solution)/shard_map/ppermute | solution.py:630
  245.3 44.5 %collective-permute-start.19 = (bf16[88,768]{1,0:T(8,128)(2,1)}, bf16[88,768]{1,0:T(8,128)(2,1)}, u32[]{:S(2)}, u32[]{:S(2)}) collective-permute-start(bf16[88,768]{1,0:T(8,128)(2,1)} %get-tuple-element.150), channel_id=1, source_target_pairs={{0,2},{1,3},{2,0},{3,1},{4,6},{5,7},{6,4},{7,5},{8,10},{9,11},{10,... | collective-permute-start | bytes 405512 | tf_op jit(solution)/shard_map/ppermute | solution.py:630
  282.9 7.8 %collective-permute-start.20 = (bf16[88,768]{1,0:T(8,128)(2,1)}, bf16[88,768]{1,0:T(8,128)(2,1)}, u32[]{:S(2)}, u32[]{:S(2)}) collective-permute-start(bf16[88,768]{1,0:T(8,128)(2,1)} %get-tuple-element.151), channel_id=1, source_target_pairs={{0,3},{1,2},{2,1},{3,0},{4,7},{5,6},{6,5},{7,4},{8,11},{9,10},{10,... | collective-permute-start | bytes 405512 | tf_op jit(solution)/shard_map/ppermute | solution.py:630
  296.2 7.9 %collective-permute-start.23 = (bf16[160,128]{1,0:T(8,128)(2,1)}, bf16[160,128]{1,0:T(8,128)(2,1)S(1)}, u32[]{:S(2)}, u32[]{:S(2)}) collective-permute-start(bf16[160,128]{1,0:T(8,128)(2,1)} %get-tuple-element.155), channel_id=1, source_target_pairs={{0,12},{4,8},{8,4},{12,0},{16,28},{20,24},{24,20},{28,16},{1,13},{... | collective-permute-start | bytes 122888 | tf_op jit(solution)/shard_map/ppermute | solution.py:630
  296.6 7.5 %collective-permute-start.24 = (bf16[160,128]{1,0:T(8,128)(2,1)}, bf16[160,128]{1,0:T(8,128)(2,1)S(1)}, u32[]{:S(2)}, u32[]{:S(2)}) collective-permute-start(bf16[160,128]{1,0:T(8,128)(2,1)} %get-tuple-element.156), channel_id=1, source_target_pairs={{0,16},{4,20},{8,24},{12,28},{16,0},{20,4},{24,8},{28,12},{1,17},{... | collective-permute-start | bytes 122888 | tf_op jit(solution)/shard_map/ppermute | solution.py:630
  299.2 8.0 %collective-permute-start.25 = (bf16[160,128]{1,0:T(8,128)(2,1)}, bf16[160,128]{1,0:T(8,128)(2,1)S(1)}, u32[]{:S(2)}, u32[]{:S(2)}) collective-permute-start(bf16[160,128]{1,0:T(8,128)(2,1)} %get-tuple-element.157), channel_id=1, source_target_pairs={{0,20},{4,16},{8,28},{12,24},{16,4},{20,0},{24,12},{28,8},{1,21},{... | collective-permute-start | bytes 122888 | tf_op jit(solution)/shard_map/ppermute | solution.py:630
  304.1 67.7 %collective-permute-start.9 = (bf16[1024,768]{1,0:T(8,128)(2,1)S(1)}, bf16[1024,768]{1,0:T(8,128)(2,1)}, u32[]{:S(2)}, u32[]{:S(2)}) collective-permute-start(bf16[1024,768]{1,0:T(8,128)(2,1)S(1)} %copy-done.3), channel_id=1, source_target_pairs={{0,1},{1,0},{2,3},{3,2},{4,5},{5,4},{6,7},{7,6},{8,9},{9,8},{10,11... | collective-permute-start | bytes 4718600 | tf_op jit(solution)/shard_map/ppermute | solution.py:630
  304.2 67.7 %collective-permute-start.11 = (bf16[1024,768]{1,0:T(8,128)(2,1)S(1)}, bf16[1024,768]{1,0:T(8,128)(2,1)}, u32[]{:S(2)}, u32[]{:S(2)}) collective-permute-start(bf16[1024,768]{1,0:T(8,128)(2,1)S(1)} %copy-done.1), channel_id=1, source_target_pairs={{0,1},{1,0},{2,3},{3,2},{4,5},{5,4},{6,7},{7,6},{8,9},{9,8},{10,11... | collective-permute-start | bytes 4718600 | tf_op jit(solution)/shard_map/ppermute | solution.py:630
  307.3 73.3 %collective-permute-start.12 = (bf16[1024,768]{1,0:T(8,128)(2,1)}, bf16[1024,768]{1,0:T(8,128)(2,1)}, u32[]{:S(2)}, u32[]{:S(2)}) collective-permute-start(bf16[1024,768]{1,0:T(8,128)(2,1)} %get-tuple-element.143.own), channel_id=1, source_target_pairs={{0,1},{1,0},{2,3},{3,2},{4,5},{5,4},{6,7},{7,6},{8,9},{9,8},{10,11... | collective-permute-start | bytes 4718600 | tf_op jit(solution)/shard_map/ppermute | solution.py:630
  307.3 73.3 %collective-permute-start.14 = (bf16[1024,768]{1,0:T(8,128)(2,1)}, bf16[1024,768]{1,0:T(8,128)(2,1)}, u32[]{:S(2)}, u32[]{:S(2)}) collective-permute-start(bf16[1024,768]{1,0:T(8,128)(2,1)} %collective-permute-done.13.two), channel_id=1, source_target_pairs={{0,1},{1,0},{2,3},{3,2},{4,5},{5,4},{6,7},{7,6},{8,9},{9,8},{10,11... | collective-permute-start | bytes 4718600 | tf_op jit(solution)/shard_map/ppermute | solution.py:630
  354.9 7.3 %collective-permute-start.36 = (bf16[1280,128]{1,0:T(8,128)(2,1)}, bf16[1280,128]{1,0:T(8,128)(2,1)S(1)}, u32[]{:S(2)}, u32[]{:S(2)}) collective-permute-start(bf16[1280,128]{1,0:T(8,128)(2,1)} %shard_map.382.own), channel_id=1, source_target_pairs={{0,2},{1,3},{2,0},{3,1},{4,6},{5,7},{6,4},{7,5},{8,10},{9,11},{10,... | collective-permute-start | bytes 983048 | tf_op jit(solution)/shard_map/ppermute | solution.py:630
  (39 other events, 686.2 us)
